TPU v7x, 512 devices: a whole 4x4x16 slice. The times are simulated.
512 devices in a mesh: lon: 64 (over z_lo, x, core), lat: 8 (over y, z_hi).
Axes of the slice: x: 4, y: 4, z: 16 (z_hi: 2, z_lo: 8; z = z_hi * 8 + z_lo), core: 2. Of those that a mesh axis runs over, the one named last changes fastest.
Arguments:
- state: bfloat16 [256, 1024, 192], P('lat', 'lon'), may hold values from -6 to 6
- land_mask: int32 [256, 1024], P('lat', 'lon'), may hold values 0 or 1
- cotangent: bfloat16 [256, 1024, 192], P('lat', 'lon'), may hold values from -6 to 6
- kernel: bfloat16 [7, 7, 192], replicated, may hold values from -0.875 to 0.875
- norm_gain: float32 [192], replicated, may hold values from 0.5 to 2
- norm_bias: float32 [192], replicated, may hold values from -3 to 3
- weight_in: bfloat16 [192, 768], replicated, may hold values from -0.4375 to 0.4375
- bias_hidden: float32 [768], replicated, may hold values from -3 to 3
- weight_out: bfloat16 [768, 192], replicated, may hold values from -0.21875 to 0.21875
- bias_out: float32 [192], replicated, may hold values from -3 to 3
- layer_scale: float32 [192], replicated, may hold values from 0.3 to 1.5
Outputs:
- block_out: bfloat16 [256, 1024, 192], P('lat', 'lon')
- grad_state: bfloat16 [256, 1024, 192], P('lat', 'lon')
- grad_kernel: float32 [7, 7, 192], replicated
- grad_norm_gain: float32 [192], replicated
- grad_norm_bias: float32 [192], replicated
- grad_weight_in: float32 [192, 768], replicated
- grad_bias_hidden: float32 [768], replicated
- grad_weight_out: float32 [768, 192], replicated
- grad_bias_out: float32 [192], replicated
- grad_layer_scale: float32 [192], replicated
All inputs are finite; a program needn't handle non-finite values. No bound on the sum of `land_mask` on one device may be relied on, other than what follows from the above.
Results may differ from a plain program's by a relative error of at most 0.0069.
Values may be sent and summed in bfloat16 or wider, within the bound.
A program may use at most 64 MiB of HBM per device.

v0:
```python
import math

import jax
import jax.numpy as jnp
from jax import lax
from jax.sharding import PartitionSpec as P

EPSILON = 1e-06


def padded_2(x, sides, width, wrap):
    for axis, dim in sides:
        peers, length = (lax.axis_size(axis), x.shape[dim])
        up = [(i, (i + 1) % peers) for i in range(peers if wrap else peers - 1)]
        down = [(j, i) for i, j in up]
        last = lax.slice_in_dim(x, length - width, length, axis=dim)
        initial = lax.slice_in_dim(x, 0, width, axis=dim)
        before = lax.ppermute(last, axis, up)
        after = lax.ppermute(initial, axis, down)
        x = jnp.concatenate([before, x, after], axis=dim)
    return x


def from_partner(value, axis, distance):
    mask = 2**distance
    pairs = [(source, source ^ mask) for source in range(lax.axis_size(axis))]
    return lax.ppermute(value, axis, pairs)


def depthwise(padded, kernel, row_count, col_count):
    running = jnp.zeros((row_count, col_count, padded.shape[2]), jnp.float32)
    for tap_row in range(7):
        for tap_col in range(7):
            window = padded[tap_row : tap_row + row_count, tap_col : tap_col + col_count].astype(
                jnp.float32
            )
            running = running + window * kernel[tap_row, tap_col].astype(jnp.float32)
    return running


def kernel_grad(padded, mixed_cot, row_count, col_count):
    cot_float = mixed_cot.astype(jnp.float32)
    pieces = []
    for tap_row in range(7):
        for tap_col in range(7):
            window = padded[tap_row : tap_row + row_count, tap_col : tap_col + col_count].astype(
                jnp.float32
            )
            pieces.append(jnp.sum(window * cot_float, axis=(0, 1)))
    return jnp.stack(pieces).reshape(7, 7, padded.shape[2])


def outer_sum(left, right):
    return lax.dot_general(
        left, right, (((0,), (0,)), ((), ())), preferred_element_type=jnp.float32
    )


def gelu_tanh(values):
    return jax.nn.gelu(values, approximate=True)


def cell_pass(
    padded,
    state,
    land_cells,
    cotangent,
    kernel,
    norm_gain,
    norm_bias,
    weight_in,
    bias_hidden,
    weight_out,
    bias_out,
    layer_scale,
):
    row_count, col_count, channels = state.shape
    mixed = depthwise(padded, kernel, row_count, col_count)
    average = jnp.mean(mixed, axis=2, keepdims=True)
    centred = mixed - average
    variance = jnp.mean(centred * centred, axis=2, keepdims=True)
    inv_std = lax.rsqrt(variance + EPSILON)
    unit_mixed = (centred * inv_std).reshape(-1, channels)
    flat_inv = inv_std.reshape(-1, 1)
    normed = (unit_mixed * norm_gain + norm_bias).astype(jnp.bfloat16)
    pre_act = jnp.dot(normed, weight_in, preferred_element_type=jnp.float32) + bias_hidden
    hidden = gelu_tanh(pre_act).astype(jnp.bfloat16)
    branch = jnp.dot(hidden, weight_out, preferred_element_type=jnp.float32) + bias_out
    sea_weight = land_cells.astype(jnp.float32).reshape(-1, 1)
    flat_state = state.reshape(-1, channels).astype(jnp.float32)
    flat_cot = cotangent.reshape(-1, channels).astype(jnp.float32)
    result = (sea_weight * (flat_state + layer_scale * branch)).astype(jnp.bfloat16)
    grad_branch = sea_weight * layer_scale * flat_cot
    branch_cot = grad_branch.astype(jnp.bfloat16)
    grad_hidden = jnp.dot(branch_cot, weight_out.T, preferred_element_type=jnp.float32)
    unused, pullback = jax.vjp(gelu_tanh, pre_act)
    grad_pre = pullback(grad_hidden)[0]
    pre_cot = grad_pre.astype(jnp.bfloat16)
    grad_normed = jnp.dot(pre_cot, weight_in.T, preferred_element_type=jnp.float32)
    grad_unit = grad_normed * norm_gain
    grad_mixed = flat_inv * (
        grad_unit
        - jnp.mean(grad_unit, axis=1, keepdims=True)
        - unit_mixed * jnp.mean(grad_unit * unit_mixed, axis=1, keepdims=True)
    )
    mixed_cot = grad_mixed.astype(jnp.bfloat16).reshape(row_count, col_count, channels)
    partials = (
        kernel_grad(padded, mixed_cot, row_count, col_count),
        jnp.sum(grad_normed * unit_mixed, axis=0),
        jnp.sum(grad_normed, axis=0),
        outer_sum(normed, pre_cot),
        jnp.sum(grad_pre, axis=0),
        outer_sum(hidden, branch_cot),
        jnp.sum(grad_branch, axis=0),
        jnp.sum(sea_weight * flat_cot * branch, axis=0),
    )
    return (result.reshape(row_count, col_count, channels), mixed_cot, partials)


def extend(field):
    row_count = field.shape[0]
    lon_wide = padded_2(field, (("lon", 1),), 3, True)
    lat_wide = padded_2(lon_wide, (("lat", 0),), 3, False)
    lower_part = lat_wide[: row_count + 3]
    top_rows = lon_wide[row_count - 3 :][::-1, ::-1]
    above_rows = lat_wide[row_count + 3 :]
    lon_count = lax.axis_size("lon")
    bit_list = list(range(lon_count.bit_length() - 1))
    mirrored = top_rows
    for bit_number in bit_list:
        mirrored = from_partner(mirrored, "lon", bit_number)
    is_top = lax.axis_index("lat") == lax.axis_size("lat") - 1
    upper_rows = jnp.where(is_top, jnp.zeros_like(mirrored), above_rows)
    fold_rows = jnp.where(is_top, mirrored, jnp.zeros_like(mirrored))
    return (lower_part, upper_rows, fold_rows)


def input_grad(mixed_cot, kernel):
    row_count, col_count, channels = mixed_cot.shape
    lower_rows, upper_rows, fold_rows = extend(mixed_cot)
    inner = jnp.concatenate([lower_rows, upper_rows], axis=0)
    flipped = kernel[::-1, ::-1]
    grad_masked = depthwise(inner, flipped, row_count, col_count)
    zero_rows = jnp.zeros((6,) + fold_rows.shape[1:], fold_rows.dtype)
    fold_part = depthwise(jnp.concatenate([zero_rows, fold_rows], axis=0), kernel, 3, col_count)
    return grad_masked.at[row_count - 3 :].add(fold_part)


def on_device(
    state,
    land_mask,
    cotangent,
    kernel,
    norm_gain,
    norm_bias,
    weight_in,
    bias_hidden,
    weight_out,
    bias_out,
    layer_scale,
):
    row_count, col_count, channels = state.shape
    masked = state * land_mask[:, :, None].astype(state.dtype)
    lower_rows, upper_rows, fold_rows = extend(masked)
    padded = jnp.concatenate([lower_rows, upper_rows + fold_rows], axis=0)
    block_out, mixed_cot, partials = cell_pass(
        padded,
        state,
        land_mask,
        cotangent,
        kernel,
        norm_gain,
        norm_bias,
        weight_in,
        bias_hidden,
        weight_out,
        bias_out,
        layer_scale,
    )
    grad_masked = input_grad(mixed_cot, kernel)
    summed = lax.psum(
        (
            partials[0],
            partials[1],
            partials[2],
            partials[3],
            partials[4],
            partials[5],
            partials[6],
            partials[7],
        ),
        ("lon", "lat"),
    )
    sea_weight = land_mask[:, :, None].astype(jnp.float32)
    grad_state = (sea_weight * (cotangent.astype(jnp.float32) + grad_masked)).astype(jnp.bfloat16)
    cell_total = row_count * lax.axis_size("lat") * col_count * lax.axis_size("lon")
    factor = 1.0 / math.sqrt(cell_total)
    scaled = tuple((part * factor for part in summed))
    return (
        block_out,
        grad_state,
        scaled[0],
        scaled[1],
        scaled[2],
        scaled[3],
        scaled[4],
        scaled[5],
        scaled[6],
        scaled[7],
    )


def solution(mesh):
    in_specs = (
        P("lat", "lon", None),
        P("lat", "lon"),
        P("lat", "lon", None),
        P(),
        P(),
        P(),
        P(),
        P(),
        P(),
        P(),
        P(),
    )
    out_specs = (
        P("lat", "lon", None),
        P("lat", "lon", None),
        P(),
        P(),
        P(),
        P(),
        P(),
        P(),
        P(),
        P(),
    )
    return jax.shard_map(
        on_device, mesh=mesh, in_specs=in_specs, out_specs=out_specs, check_vma=False
    )
```

profile of v0, /device:TPU:1, one launch (start us, length us, event | category | flops | bytes accessed | tf_op | source)
XLA Modules:
  0.0 627.4 jit_solution(16473069604779964397)
XLA Ops:
  7.3 0.8 fusion.146
  8.1 1.1 broadcast_multiply_fusion.2
  9.3 4.5 collective-permute-start
  13.8 6.2 collective-permute-start.1
  20.0 0.9 collective-permute-done.1
  21.1 13.4 %collective-permute-start.4 = (bf16[3,22,192]{2,1,0:T(8,128)(2,1)S(1)}, bf16[3,22,192]{2,1,0:T(8,128)(2,1)S(1)}, u32[]{:S(2)}, u32[]{:S(2)}) collective-permute-start(bf16[3,22,192]{2,1,0:T(8,128)(2,1)S(1)} %rev.7), channel_id=1, source_target_pairs={{0,8},{8,0},{16,24},{24,16},{32,40},{40,32},{48,56},{56,48},{64,72... | collective-permute-start | bytes 76040 | tf_op jit(solution)/shard_map/ppermute | solution.py:27
  34.4 0.8 collective-permute-done.4
  35.3 1.9 collective-permute-start.5
  37.2 2.8 collective-permute-done.5
  40.0 1.9 collective-permute-start.6
  42.1 4.1 collective-permute-done.6
  46.2 1.9 collective-permute-start.7
  48.3 2.6 collective-permute-done.7
  50.9 1.9 collective-permute-start.8
  52.8 0.6 slice_convert_fusion.46
  53.4 1.3 collective-permute-start.3
  54.7 1.9 collective-permute-done.8
  56.6 7.0 %collective-permute-start.9 = (bf16[3,22,192]{2,1,0:T(8,128)(2,1)S(1)}, bf16[3,22,192]{2,1,0:T(8,128)(2,1)S(1)}, u32[]{:S(2)}, u32[]{:S(2)}) collective-permute-start(bf16[3,22,192]{2,1,0:T(8,128)(2,1)S(1)} %collective-permute-done.8), channel_id=1, source_target_pairs={{0,256},{8,264},{16,272},{24,280},{32,288},{40,296},{48,304},{56,3... | collective-permute-start | bytes 76040 | tf_op jit(solution)/shard_map/ppermute | solution.py:27
  63.6 1.4 add_multiply_fusion
  65.2 0.9 copy.36
  66.2 12.7 %collective-permute-start.2 = (bf16[3,22,192]{2,1,0:T(8,128)(2,1)S(1)}, bf16[3,22,192]{2,1,0:T(8,128)(2,1)S(1)}, u32[]{:S(2)}, u32[]{:S(2)}) collective-permute-start(bf16[3,22,192]{2,1,0:T(8,128)(2,1)S(1)} %get-tuple-element.110), channel_id=1, source_target_pairs={{0,1},{1,2},{2,3},{3,4},{4,5},{5,6},{6,7},{8,9},{9,10},{10,11},{11... | collective-permute-start | bytes 76040 | tf_op jit(solution)/shard_map/ppermute | solution.py:18
  78.9 1.0 collective-permute-done.2
  80.5 5.1 fusion.142
  86.5 0.8 multiply_convert_fusion
  87.5 2.0 fusion.147
  89.4 1.2 multiply_reduce_fusion.3
  90.6 0.8 multiply_convert_fusion.2
  91.4 1.1 copy.42
  92.5 1.7 fusion.99
  94.2 1.7 fusion.127
  96.0 7.1 %collective-permute-start.10 = (bf16[32,3,192]{2,1,0:T(4,128)(2,1)S(1)}, bf16[32,3,192]{2,1,0:T(4,128)(2,1)S(1)}, u32[]{:S(2)}, u32[]{:S(2)}) collective-permute-start(bf16[32,3,192]{2,1,0:T(4,128)(2,1)S(1)} %get-tuple-element.113), channel_id=1, source_target_pairs={{0,8},{8,16},{16,24},{24,32},{32,40},{40,48},{48,56},{56,64},{64,7... | collective-permute-start | bytes 110600 | tf_op jit(solution)/shard_map/ppermute | solution.py:18
  103.1 1.9 collective-permute-start.11
  105.0 1.8 multiply_reduce_fusion.2
  106.9 1.2 fusion.141
  108.1 0.6 collective-permute-done.11
  108.8 11.0 %collective-permute-start.14 = (bf16[3,22,192]{2,1,0:T(8,128)(2,1)S(1)}, bf16[3,22,192]{2,1,0:T(8,128)(2,1)S(1)}, u32[]{:S(2)}, u32[]{:S(2)}) collective-permute-start(bf16[3,22,192]{2,1,0:T(8,128)(2,1)S(1)} %rev.8), channel_id=1, source_target_pairs={{0,8},{8,0},{16,24},{24,16},{32,40},{40,32},{48,56},{56,48},{64,72... | collective-permute-start | bytes 76040 | tf_op jit(solution)/shard_map/ppermute | solution.py:27
  119.8 2.4 fusion.128
  122.2 2.2 collective-permute-start.15
  124.4 0.8 fusion.106
  125.2 1.3 collective-permute-start.13
  126.5 0.5 collective-permute-done.15
  127.0 1.9 collective-permute-start.16
  128.9 0.5 fusion.109
  129.4 0.8 copy.37
  130.6 5.0 stack.199
  135.6 12.9 %collective-permute-start.12 = (bf16[3,22,192]{2,1,0:T(8,128)(2,1)S(1)}, bf16[3,22,192]{2,1,0:T(8,128)(2,1)S(1)}, u32[]{:S(2)}, u32[]{:S(2)}) collective-permute-start(bf16[3,22,192]{2,1,0:T(8,128)(2,1)S(1)} %get-tuple-element.105), channel_id=1, source_target_pairs={{0,1},{1,2},{2,3},{3,4},{4,5},{5,6},{6,7},{8,9},{9,10},{10,11},{11... | collective-permute-start | bytes 76040 | tf_op jit(solution)/shard_map/ppermute | solution.py:18
  148.6 1.9 collective-permute-start.17
  150.5 2.7 collective-permute-done.17
  153.3 1.9 collective-permute-start.18
  155.5 3.9 collective-permute-done.18
  159.4 8.5 %collective-permute-start.19 = (bf16[3,22,192]{2,1,0:T(8,128)(2,1)S(1)}, bf16[3,22,192]{2,1,0:T(8,128)(2,1)S(1)}, u32[]{:S(2)}, u32[]{:S(2)}) collective-permute-start(bf16[3,22,192]{2,1,0:T(8,128)(2,1)S(1)} %collective-permute-done.18), channel_id=1, source_target_pairs={{0,256},{8,264},{16,272},{24,280},{32,288},{40,296},{48,304},{56,3... | collective-permute-start | bytes 76040 | tf_op jit(solution)/shard_map/ppermute | solution.py:27
  168.3 4.9 fusion.78
  173.2 0.8 fusion.140
  174.0 1.6 multiply_reduce_fusion
  175.6 113.8 %all-reduce.1 = (f32[7,7,192]{2,1,0:T(8,128)S(1)}, f32[192]{0:T(256)S(1)}, f32[192]{0:T(256)S(1)}, f32[768]{0:T(1024)S(1)}, f32[192]{0:T(256)S(1)}, /*index=5*/f32[192]{0:T(256)S(1)}) all-reduce(f32[7,7,192]{2,1,0:T(8,128)S(1)} %reshape.125, f32[192]{0:T(256)} %get-tuple-element.32, ...), channel_id=1, replica_groups=mesh['lon'=64,'lat'=8] {'lon','lat'}, use_global_device_ids=true, to_apply=%region_53.54 | all-reduce | flops 10944 | bytes 87552 | tf_op jit(solution)/shard_map/psum | solution.py:181
  289.4 0.6 broadcast_multiply_fusion.11
  290.0 0.6 broadcast_multiply_fusion.10
  290.6 0.6 broadcast_multiply_fusion.9
  291.1 0.6 broadcast_multiply_fusion.8
  291.7 0.6 broadcast_multiply_fusion.5
  292.3 0.6 broadcast_multiply_fusion.3
  292.9 324.8 %all-reduce.5.cloned.1.call-done = (f32[192,768]{1,0:T(8,128)}, f32[768,192]{0,1:T(8,128)}) async-done(((f32[192,768]{1,0:T(8,128)}, f32[768,192]{0,1:T(8,128)}), (f32[192,768]{1,0:T(8,128)}, f32[768,192]{0,1:T(8,128)})) %all-reduce.5.cloned.1.call-update) | async-done | bytes 1179664 | tf_op jit(solution)/shard_map/psum | solution.py:181
  617.7 2.0 broadcast_multiply_fusion.1
  619.7 0.9 broadcast_multiply_fusion
  (224 shorter events, 2.7 us)
Async XLA Ops:
  7.2 79.3 %copy-start = (bf16[192,768]{1,0:T(8,128)(2,1)S(1)}, bf16[192,768]{1,0:T(8,128)(2,1)}, u32[]{:S(2)}) copy-start(bf16[192,768]{1,0:T(8,128)(2,1)} %param.19) | copy-start | bytes 884740
  7.2 57.9 %copy-start.3 = (bf16[32,16,192]{2,1,0:T(8,128)(2,1)S(1)}, bf16[32,16,192]{2,1,0:T(8,128)(2,1)}, u32[]{:S(2)}) copy-start(bf16[32,16,192]{2,1,0:T(8,128)(2,1)} %param.15) | copy-start | bytes 589828
  7.2 610.5 %all-reduce.5.cloned.1.call-start = ((), (), s32[]{:S(2)}) async-start(), calls=%async_computation | async-start | bytes 2359296 | tf_op jit(solution)/shard_map/psum | solution.py:181
  9.3 10.7 %collective-permute-start = (bf16[32,3,192]{2,1,0:T(4,128)(2,1)S(1)}, bf16[32,3,192]{2,1,0:T(4,128)(2,1)S(1)}, u32[]{:S(2)}, u32[]{:S(2)}) collective-permute-start(bf16[32,3,192]{2,1,0:T(4,128)(2,1)S(1)} %get-tuple-element.115), channel_id=1, source_target_pairs={{0,8},{8,16},{16,24},{24,32},{32,40},{40,48},{48,56},{56,64},{64,7... | collective-permute-start | bytes 110600 | tf_op jit(solution)/shard_map/ppermute | solution.py:18
  13.8 7.1 %collective-permute-start.1 = (bf16[32,3,192]{2,1,0:T(4,128)(2,1)S(1)}, bf16[32,3,192]{2,1,0:T(4,128)(2,1)S(1)}, u32[]{:S(2)}, u32[]{:S(2)}) collective-permute-start(bf16[32,3,192]{2,1,0:T(4,128)(2,1)S(1)} %get-tuple-element.116), channel_id=1, source_target_pairs={{8,0},{16,8},{24,16},{32,24},{40,32},{48,40},{56,48},{64,56},{72,6... | collective-permute-start | bytes 110600 | tf_op jit(solution)/shard_map/ppermute | solution.py:19
  21.1 14.2 %collective-permute-start.4 = (bf16[3,22,192]{2,1,0:T(8,128)(2,1)S(1)}, bf16[3,22,192]{2,1,0:T(8,128)(2,1)S(1)}, u32[]{:S(2)}, u32[]{:S(2)}) collective-permute-start(bf16[3,22,192]{2,1,0:T(8,128)(2,1)S(1)} %rev.7), channel_id=1, source_target_pairs={{0,8},{8,0},{16,24},{24,16},{32,40},{40,32},{48,56},{56,48},{64,72... | collective-permute-start | bytes 76040 | tf_op jit(solution)/shard_map/ppermute | solution.py:27
  35.3 4.7 collective-permute-start.5
  40.0 6.2 collective-permute-start.6
  41.9 38.2 %copy-start.10 = (f32[1,1,192]{2,1,0:T(1,128)}, f32[1,1,192]{2,1,0:T(1,128)S(1)}, u32[]{:S(2)}) copy-start(f32[1,1,192]{2,1,0:T(1,128)S(1)} %get-tuple-element.125) | copy-start | bytes 2308
  41.9 38.2 %copy-start.12 = (f32[1,1,192]{2,1,0:T(1,128)}, f32[1,1,192]{2,1,0:T(1,128)S(1)}, u32[]{:S(2)}) copy-start(f32[1,1,192]{2,1,0:T(1,128)S(1)} %get-tuple-element.126) | copy-start | bytes 2308
  41.9 38.2 %copy-start.14 = (f32[1,1,192]{2,1,0:T(1,128)}, f32[1,1,192]{2,1,0:T(1,128)S(1)}, u32[]{:S(2)}) copy-start(f32[1,1,192]{2,1,0:T(1,128)S(1)} %get-tuple-element.127) | copy-start | bytes 2308
  42.0 38.2 %copy-start.16 = (f32[1,1,192]{2,1,0:T(1,128)}, f32[1,1,192]{2,1,0:T(1,128)S(1)}, u32[]{:S(2)}) copy-start(f32[1,1,192]{2,1,0:T(1,128)S(1)} %get-tuple-element.128) | copy-start | bytes 2308
  42.0 38.2 %copy-start.18 = (f32[1,1,192]{2,1,0:T(1,128)}, f32[1,1,192]{2,1,0:T(1,128)S(1)}, u32[]{:S(2)}) copy-start(f32[1,1,192]{2,1,0:T(1,128)S(1)} %get-tuple-element.129) | copy-start | bytes 2308
  42.0 38.2 %copy-start.20 = (f32[1,1,192]{2,1,0:T(1,128)}, f32[1,1,192]{2,1,0:T(1,128)S(1)}, u32[]{:S(2)}) copy-start(f32[1,1,192]{2,1,0:T(1,128)S(1)} %get-tuple-element.130) | copy-start | bytes 2308
  42.0 38.2 %copy-start.22 = (f32[1,1,192]{2,1,0:T(1,128)}, f32[1,1,192]{2,1,0:T(1,128)S(1)}, u32[]{:S(2)}) copy-start(f32[1,1,192]{2,1,0:T(1,128)S(1)} %get-tuple-element.131) | copy-start | bytes 2308
  42.0 38.2 %copy-start.24 = (f32[1,1,192]{2,1,0:T(1,128)}, f32[1,1,192]{2,1,0:T(1,128)S(1)}, u32[]{:S(2)}) copy-start(f32[1,1,192]{2,1,0:T(1,128)S(1)} %get-tuple-element.132) | copy-start | bytes 2308
  42.0 38.2 %copy-start.26 = (f32[1,1,192]{2,1,0:T(1,128)}, f32[1,1,192]{2,1,0:T(1,128)S(1)}, u32[]{:S(2)}) copy-start(f32[1,1,192]{2,1,0:T(1,128)S(1)} %get-tuple-element.133) | copy-start | bytes 2308
  42.0 38.2 %copy-start.28 = (f32[1,1,192]{2,1,0:T(1,128)}, f32[1,1,192]{2,1,0:T(1,128)S(1)}, u32[]{:S(2)}) copy-start(f32[1,1,192]{2,1,0:T(1,128)S(1)} %get-tuple-element.134) | copy-start | bytes 2308
  42.0 38.2 %copy-start.30 = (f32[1,1,192]{2,1,0:T(1,128)}, f32[1,1,192]{2,1,0:T(1,128)S(1)}, u32[]{:S(2)}) copy-start(f32[1,1,192]{2,1,0:T(1,128)S(1)} %get-tuple-element.135) | copy-start | bytes 2308
  42.0 38.2 %copy-start.32 = (f32[1,1,192]{2,1,0:T(1,128)}, f32[1,1,192]{2,1,0:T(1,128)S(1)}, u32[]{:S(2)}) copy-start(f32[1,1,192]{2,1,0:T(1,128)S(1)} %get-tuple-element.136) | copy-start | bytes 2308
  42.0 38.2 %copy-start.34 = (f32[1,1,192]{2,1,0:T(1,128)}, f32[1,1,192]{2,1,0:T(1,128)S(1)}, u32[]{:S(2)}) copy-start(f32[1,1,192]{2,1,0:T(1,128)S(1)} %get-tuple-element.137) | copy-start | bytes 2308
  42.1 38.2 %copy-start.42 = (f32[1,1,192]{2,1,0:T(1,128)}, f32[1,1,192]{2,1,0:T(1,128)S(1)}, u32[]{:S(2)}) copy-start(f32[1,1,192]{2,1,0:T(1,128)S(1)} %get-tuple-element.119) | copy-start | bytes 2308
  46.2 4.7 collective-permute-start.7
  50.9 5.7 collective-permute-start.8
  53.4 25.5 %collective-permute-start.3 = (bf16[3,22,192]{2,1,0:T(8,128)(2,1)S(1)}, bf16[3,22,192]{2,1,0:T(8,128)(2,1)S(1)}, u32[]{:S(2)}, u32[]{:S(2)}) collective-permute-start(bf16[3,22,192]{2,1,0:T(8,128)(2,1)S(1)} %get-tuple-element.109), channel_id=1, source_target_pairs={{1,0},{2,1},{3,2},{4,3},{5,4},{6,5},{7,6},{9,8},{10,9},{11,10},{12... | collective-permute-start | bytes 76040 | tf_op jit(solution)/shard_map/ppermute | solution.py:19
  56.6 22.3 %collective-permute-start.9 = (bf16[3,22,192]{2,1,0:T(8,128)(2,1)S(1)}, bf16[3,22,192]{2,1,0:T(8,128)(2,1)S(1)}, u32[]{:S(2)}, u32[]{:S(2)}) collective-permute-start(bf16[3,22,192]{2,1,0:T(8,128)(2,1)S(1)} %collective-permute-done.8), channel_id=1, source_target_pairs={{0,256},{8,264},{16,272},{24,280},{32,288},{40,296},{48,304},{56,3... | collective-permute-start | bytes 76040 | tf_op jit(solution)/shard_map/ppermute | solution.py:27
  66.2 13.7 %collective-permute-start.2 = (bf16[3,22,192]{2,1,0:T(8,128)(2,1)S(1)}, bf16[3,22,192]{2,1,0:T(8,128)(2,1)S(1)}, u32[]{:S(2)}, u32[]{:S(2)}) collective-permute-start(bf16[3,22,192]{2,1,0:T(8,128)(2,1)S(1)} %get-tuple-element.110), channel_id=1, source_target_pairs={{0,1},{1,2},{2,3},{3,4},{4,5},{5,6},{6,7},{8,9},{9,10},{10,11},{11... | collective-permute-start | bytes 76040 | tf_op jit(solution)/shard_map/ppermute | solution.py:18
  96.0 12.1 %collective-permute-start.10 = (bf16[32,3,192]{2,1,0:T(4,128)(2,1)S(1)}, bf16[32,3,192]{2,1,0:T(4,128)(2,1)S(1)}, u32[]{:S(2)}, u32[]{:S(2)}) collective-permute-start(bf16[32,3,192]{2,1,0:T(4,128)(2,1)S(1)} %get-tuple-element.113), channel_id=1, source_target_pairs={{0,8},{8,16},{16,24},{24,32},{32,40},{40,48},{48,56},{56,64},{64,7... | collective-permute-start | bytes 110600 | tf_op jit(solution)/shard_map/ppermute | solution.py:18
  103.1 5.6 collective-permute-start.11
  108.8 13.4 %collective-permute-start.14 = (bf16[3,22,192]{2,1,0:T(8,128)(2,1)S(1)}, bf16[3,22,192]{2,1,0:T(8,128)(2,1)S(1)}, u32[]{:S(2)}, u32[]{:S(2)}) collective-permute-start(bf16[3,22,192]{2,1,0:T(8,128)(2,1)S(1)} %rev.8), channel_id=1, source_target_pairs={{0,8},{8,0},{16,24},{24,16},{32,40},{40,32},{48,56},{56,48},{64,72... | collective-permute-start | bytes 76040 | tf_op jit(solution)/shard_map/ppermute | solution.py:27
  122.2 4.8 collective-permute-start.15
  125.2 25.3 %collective-permute-start.13 = (bf16[3,22,192]{2,1,0:T(8,128)(2,1)S(1)}, bf16[3,22,192]{2,1,0:T(8,128)(2,1)S(1)}, u32[]{:S(2)}, u32[]{:S(2)}) collective-permute-start(bf16[3,22,192]{2,1,0:T(8,128)(2,1)S(1)} %get-tuple-element.106), channel_id=1, source_target_pairs={{1,0},{2,1},{3,2},{4,3},{5,4},{6,5},{7,6},{9,8},{10,9},{11,10},{12... | collective-permute-start | bytes 76040 | tf_op jit(solution)/shard_map/ppermute | solution.py:19
  127.0 21.6 %collective-permute-start.16 = (bf16[3,22,192]{2,1,0:T(8,128)(2,1)S(1)}, bf16[3,22,192]{2,1,0:T(8,128)(2,1)S(1)}, u32[]{:S(2)}, u32[]{:S(2)}) collective-permute-start(bf16[3,22,192]{2,1,0:T(8,128)(2,1)S(1)} %collective-permute-done.15), channel_id=1, source_target_pairs={{0,32},{8,40},{16,48},{24,56},{32,0},{40,8},{48,16},{56,24},{64,96... | collective-permute-start | bytes 76040 | tf_op jit(solution)/shard_map/ppermute | solution.py:27
  130.3 37.7 %copy-start.19 = (f32[1,1,192]{2,1,0:T(1,128)S(1)}, f32[1,1,192]{2,1,0:T(1,128)}, u32[]{:S(2)}) copy-start(f32[1,1,192]{2,1,0:T(1,128)} %copy-done.18) | copy-start | bytes 2308
  130.3 37.7 %copy-start.21 = (f32[1,1,192]{2,1,0:T(1,128)S(1)}, f32[1,1,192]{2,1,0:T(1,128)}, u32[]{:S(2)}) copy-start(f32[1,1,192]{2,1,0:T(1,128)} %copy-done.20) | copy-start | bytes 2308
  130.3 37.7 %copy-start.23 = (f32[1,1,192]{2,1,0:T(1,128)S(1)}, f32[1,1,192]{2,1,0:T(1,128)}, u32[]{:S(2)}) copy-start(f32[1,1,192]{2,1,0:T(1,128)} %copy-done.22) | copy-start | bytes 2308
  130.3 37.7 %copy-start.25 = (f32[1,1,192]{2,1,0:T(1,128)S(1)}, f32[1,1,192]{2,1,0:T(1,128)}, u32[]{:S(2)}) copy-start(f32[1,1,192]{2,1,0:T(1,128)} %copy-done.24) | copy-start | bytes 2308
  130.3 37.7 %copy-start.27 = (f32[1,1,192]{2,1,0:T(1,128)S(1)}, f32[1,1,192]{2,1,0:T(1,128)}, u32[]{:S(2)}) copy-start(f32[1,1,192]{2,1,0:T(1,128)} %copy-done.26) | copy-start | bytes 2308
  130.3 37.7 %copy-start.29 = (f32[1,1,192]{2,1,0:T(1,128)S(1)}, f32[1,1,192]{2,1,0:T(1,128)}, u32[]{:S(2)}) copy-start(f32[1,1,192]{2,1,0:T(1,128)} %copy-done.28) | copy-start | bytes 2308
  130.4 37.7 %copy-start.31 = (f32[1,1,192]{2,1,0:T(1,128)S(1)}, f32[1,1,192]{2,1,0:T(1,128)}, u32[]{:S(2)}) copy-start(f32[1,1,192]{2,1,0:T(1,128)} %copy-done.30) | copy-start | bytes 2308
  130.4 37.7 %copy-start.33 = (f32[1,1,192]{2,1,0:T(1,128)S(1)}, f32[1,1,192]{2,1,0:T(1,128)}, u32[]{:S(2)}) copy-start(f32[1,1,192]{2,1,0:T(1,128)} %copy-done.32) | copy-start | bytes 2308
  130.4 37.7 %copy-start.35 = (f32[1,1,192]{2,1,0:T(1,128)S(1)}, f32[1,1,192]{2,1,0:T(1,128)}, u32[]{:S(2)}) copy-start(f32[1,1,192]{2,1,0:T(1,128)} %copy-done.34) | copy-start | bytes 2308
  130.4 37.7 %copy-start.37 = (f32[1,1,192]{2,1,0:T(1,128)S(1)}, f32[1,1,192]{2,1,0:T(1,128)}, u32[]{:S(2)}) copy-start(f32[1,1,192]{2,1,0:T(1,128)} %copy-done.36) | copy-start | bytes 2308
  130.4 37.7 %copy-start.39 = (f32[1,1,192]{2,1,0:T(1,128)S(1)}, f32[1,1,192]{2,1,0:T(1,128)}, u32[]{:S(2)}) copy-start(f32[1,1,192]{2,1,0:T(1,128)} %copy-done.38) | copy-start | bytes 2308
  130.4 37.7 %copy-start.41 = (f32[1,1,192]{2,1,0:T(1,128)S(1)}, f32[1,1,192]{2,1,0:T(1,128)}, u32[]{:S(2)}) copy-start(f32[1,1,192]{2,1,0:T(1,128)} %copy-done.40) | copy-start | bytes 2308
  130.4 37.7 %copy-start.43 = (f32[1,1,192]{2,1,0:T(1,128)S(1)}, f32[1,1,192]{2,1,0:T(1,128)}, u32[]{:S(2)}) copy-start(f32[1,1,192]{2,1,0:T(1,128)} %copy-done.42) | copy-start | bytes 2308
  130.4 37.7 %copy-start.45 = (f32[1,1,192]{2,1,0:T(1,128)S(1)}, f32[1,1,192]{2,1,0:T(1,128)}, u32[]{:S(2)}) copy-start(f32[1,1,192]{2,1,0:T(1,128)} %copy-done.44) | copy-start | bytes 2308
  130.4 37.7 %copy-start.47 = (f32[1,1,192]{2,1,0:T(1,128)S(1)}, f32[1,1,192]{2,1,0:T(1,128)}, u32[]{:S(2)}) copy-start(f32[1,1,192]{2,1,0:T(1,128)} %copy-done.46) | copy-start | bytes 2308
  130.4 37.7 %copy-start.49 = (f32[1,1,192]{2,1,0:T(1,128)S(1)}, f32[1,1,192]{2,1,0:T(1,128)}, u32[]{:S(2)}) copy-start(f32[1,1,192]{2,1,0:T(1,128)} %copy-done.48) | copy-start | bytes 2308
  130.5 37.7 %copy-start.51 = (f32[1,1,192]{2,1,0:T(1,128)S(1)}, f32[1,1,192]{2,1,0:T(1,128)}, u32[]{:S(2)}) copy-start(f32[1,1,192]{2,1,0:T(1,128)} %copy-done.50) | copy-start | bytes 2308
  130.5 37.7 %copy-start.53 = (f32[1,1,192]{2,1,0:T(1,128)S(1)}, f32[1,1,192]{2,1,0:T(1,128)}, u32[]{:S(2)}) copy-start(f32[1,1,192]{2,1,0:T(1,128)} %copy-done.52) | copy-start | bytes 2308
  130.5 37.7 %copy-start.55 = (f32[1,1,192]{2,1,0:T(1,128)S(1)}, f32[1,1,192]{2,1,0:T(1,128)}, u32[]{:S(2)}) copy-start(f32[1,1,192]{2,1,0:T(1,128)} %copy-done.54) | copy-start | bytes 2308
  130.5 37.7 %copy-start.57 = (f32[1,1,192]{2,1,0:T(1,128)S(1)}, f32[1,1,192]{2,1,0:T(1,128)}, u32[]{:S(2)}) copy-start(f32[1,1,192]{2,1,0:T(1,128)} %copy-done.56) | copy-start | bytes 2308
  130.5 37.7 %copy-start.59 = (f32[1,1,192]{2,1,0:T(1,128)S(1)}, f32[1,1,192]{2,1,0:T(1,128)}, u32[]{:S(2)}) copy-start(f32[1,1,192]{2,1,0:T(1,128)} %copy-done.58) | copy-start | bytes 2308
  130.5 37.7 %copy-start.61 = (f32[1,1,192]{2,1,0:T(1,128)S(1)}, f32[1,1,192]{2,1,0:T(1,128)}, u32[]{:S(2)}) copy-start(f32[1,1,192]{2,1,0:T(1,128)} %copy-done.60) | copy-start | bytes 2308
  130.5 37.7 %copy-start.63 = (f32[1,1,192]{2,1,0:T(1,128)S(1)}, f32[1,1,192]{2,1,0:T(1,128)}, u32[]{:S(2)}) copy-start(f32[1,1,192]{2,1,0:T(1,128)} %copy-done.62) | copy-start | bytes 2308
  130.5 37.7 %copy-start.65 = (f32[1,1,192]{2,1,0:T(1,128)S(1)}, f32[1,1,192]{2,1,0:T(1,128)}, u32[]{:S(2)}) copy-start(f32[1,1,192]{2,1,0:T(1,128)} %copy-done.64) | copy-start | bytes 2308
  130.5 37.7 %copy-start.67 = (f32[1,1,192]{2,1,0:T(1,128)S(1)}, f32[1,1,192]{2,1,0:T(1,128)}, u32[]{:S(2)}) copy-start(f32[1,1,192]{2,1,0:T(1,128)} %copy-done.66) | copy-start | bytes 2308
  130.5 37.7 %copy-start.69 = (f32[1,1,192]{2,1,0:T(1,128)S(1)}, f32[1,1,192]{2,1,0:T(1,128)}, u32[]{:S(2)}) copy-start(f32[1,1,192]{2,1,0:T(1,128)} %copy-done.68) | copy-start | bytes 2308
  130.6 37.7 %copy-start.71 = (f32[1,1,192]{2,1,0:T(1,128)S(1)}, f32[1,1,192]{2,1,0:T(1,128)}, u32[]{:S(2)}) copy-start(f32[1,1,192]{2,1,0:T(1,128)} %copy-done.70) | copy-start | bytes 2308
  135.6 19.6 %collective-permute-start.12 = (bf16[3,22,192]{2,1,0:T(8,128)(2,1)S(1)}, bf16[3,22,192]{2,1,0:T(8,128)(2,1)S(1)}, u32[]{:S(2)}, u32[]{:S(2)}) collective-permute-start(bf16[3,22,192]{2,1,0:T(8,128)(2,1)S(1)} %get-tuple-element.105), channel_id=1, source_target_pairs={{0,1},{1,2},{2,3},{3,4},{4,5},{5,6},{6,7},{8,9},{9,10},{10,11},{11... | collective-permute-start | bytes 76040 | tf_op jit(solution)/shard_map/ppermute | solution.py:18
  148.6 4.7 collective-permute-start.17
  153.3 6.1 collective-permute-start.18
  159.4 13.8 %collective-permute-start.19 = (bf16[3,22,192]{2,1,0:T(8,128)(2,1)S(1)}, bf16[3,22,192]{2,1,0:T(8,128)(2,1)S(1)}, u32[]{:S(2)}, u32[]{:S(2)}) collective-permute-start(bf16[3,22,192]{2,1,0:T(8,128)(2,1)S(1)} %collective-permute-done.18), channel_id=1, source_target_pairs={{0,256},{8,264},{16,272},{24,280},{32,288},{40,296},{48,304},{56,3... | collective-permute-start | bytes 76040 | tf_op jit(solution)/shard_map/ppermute | solution.py:27
  (51 other events, 1324.3 us)
Sparse Core Ops, SparseCore 0:
  135.8 481.8 all-reduce.4
where the time goes:
time: 629 us; the launch traced here: 627 us
  waiting for transfers between devices  347 us (55%)
  blocking collectives  114 us (18%)
  starting transfers between devices  103 us (16%)
  other arithmetic  29.1 us (5%)
  between operations  15.8 us (3%)
  matrix products  9.39 us (1%)
  local copies, waits for them, and re-layouts  9.3 us (1%)
    psum x1, waiting for transfers between devices, on_device(): lax.psum((partials[0], partials[1], partials[2], partials[3], partials[4]...  325 us
    psum x1, blocking collectives, on_device(): lax.psum((partials[0], partials[1], partials[2], partials[3], partials[4]...  114 us
    ppermute x12, starting transfers between devices, from_partner(): return lax.ppermute(value, axis, pairs)  55.5 us
    ppermute x4, starting transfers between devices, padded_2(): before = lax.ppermute(last, axis, up)  37.2 us
    ppermute x12, waiting for transfers between devices, from_partner(): return lax.ppermute(value, axis, pairs)  19.4 us
  transfers between devices with their start and end apart: 21, of which 12 were waited for; matrix products, arithmetic and copies ran while one was open for 4% of the time, Pallas kernels for 0%

commit v1 on v0

v1 whole, which is shorter than its diff:
```python
import functools
import math

import jax
import jax.numpy as jnp
from jax import lax
from jax.experimental import pallas as pl
from jax.experimental.pallas import tpu as pltpu
from jax.sharding import PartitionSpec as P

EPSILON = 1e-06
MESH = pl.DeviceIdType.MESH
F32 = jnp.float32
BF16 = jnp.bfloat16

ROWS, COLS, C, HID = 32, 16, 192, 768
CELLS = ROWS * COLS
PADR, WIDE = ROWS + 6, 32
WROWS = C * HID // 128
SROWS = 64
TOT = WROWS + 2 * SROWS
GELU_A = math.sqrt(2.0 / math.pi)
GELU_B = 0.044715


def groups(nlon, nlat):
    px = 4 if nlon >= 64 else 2
    nzl = nlon // (2 * px)
    nzh = 2 if nlat >= 8 else 1
    return px, nzl, nzh, nlat // nzh


def one_hot(shape, pick):
    a = lax.broadcasted_iota(jnp.int32, shape, 0)
    b = lax.broadcasted_iota(jnp.int32, shape, 1)
    return pick(a, b).astype(F32).astype(BF16)


def dot(a, b, contract=((1,), (0,))):
    return lax.dot_general(a, b, (contract, ((), ())), preferred_element_type=F32)


def main_kernel(
    nlon,
    nlat,
    state,
    mask,
    cot,
    kern,
    gain,
    nbias,
    w_in,
    b_hid,
    w_out,
    b_out,
    scale,
    block_out,
    grad_state,
    total,
    pad,
    shifted,
    padq,
    shiftq,
    taps,
    maskb,
    normed_s,
    precot_s,
    hidden_s,
    bcot_s,
    mcot_s,
    sums,
    sumh,
    small,
    csend,
    crecv,
    rsend,
    rrecv,
    wbuf,
    wrecv,
    psum,
    pay,
    xrecv,
    zacc,
    zrecv,
    ztot,
    abuf,
    fin,
    col_s,
    col_r,
    row_s,
    row_r,
    core_s,
    core_r,
    xs,
    xr,
    zs,
    zr,
    zas,
    zar,
    xas,
    xar,
):
    px, nzl, nzh, py = groups(nlon, nlat)
    nplane, nz = px * py, nzl * nzh
    chunk = TOT // nplane
    zrows = max(8, -(-chunk // nz // 8) * 8)
    if zrows * nz < chunk:
        zrows += 8
    owners = chunk // zrows

    lon = lax.axis_index("lon")
    lat = lax.axis_index("lat")
    core = lon % 2
    x = (lon // 2) % px
    zl = lon // (2 * px)
    zh = lat % nzh
    y = lat // nzh
    plane = y * px + x
    zi = zh * nzl + zl
    is_top = lat == nlat - 1
    has_south = lat > 0

    def device(la, lo):
        return {"lon": lo, "lat": la}

    east = device(lat, (lon + 1) % nlon)
    west = device(lat, (lon + nlon - 1) % nlon)
    north = device(
        jnp.where(is_top, lat, (lat + 1) % nlat), jnp.where(is_top, nlon - 1 - lon, lon)
    )
    south = device((lat + nlat - 1) % nlat, lon)
    pair = device(lat, lon + 1 - 2 * core)

    def in_plane(k):
        return device((k // px) * nzh + zh, zl * (2 * px) + (k % px) * 2 + core)

    def in_z(k):
        return device(y * nzh + k // nzl, (k % nzl) * (2 * px) + x * 2 + core)

    barrier = pltpu.get_barrier_semaphore()

    def hello(target):
        pl.semaphore_signal(barrier, inc=1, device_id=target, device_id_type=MESH)

    hello(east)
    hello(west)
    hello(north)
    hello(pair)

    @pl.when(has_south)
    def _():
        hello(south)

    @pl.loop(1, nplane)
    def _(d):
        hello(in_plane((plane + d) % nplane))

    @pl.loop(1, nz)
    def _(d):
        hello(in_z((zi + d) % nz))

    for a in range(7):
        k7 = kern[a].astype(F32)
        for b in range(7):
            taps[a * 7 + b] = jnp.broadcast_to(k7[b : b + 1], (8, C))
    sums[...] = jnp.zeros_like(sums)
    sumh[...] = jnp.zeros_like(sumh)
    small[...] = jnp.zeros_like(small)
    by_row = one_hot((CELLS, ROWS), lambda a, b: a // COLS == b)
    by_col = one_hot((CELLS, COLS), lambda a, b: a % COLS == b).astype(F32)
    sea = dot(by_row, mask[...].astype(F32).astype(BF16), ((1,), (1,))) * by_col
    maskb[...] = dot(sea.astype(BF16), jnp.ones((COLS, C), BF16)).reshape(ROWS, COLS, C)
    own = (state[...].astype(F32) * maskb[...]).reshape(ROWS, COLS, C)
    pad[3 : 3 + ROWS, 8:24, :] = own

    east_pick = one_hot((96, CELLS), lambda a, b: (a // 3) * COLS + 13 + a % 3 == b)
    west_pick = one_hot((96, CELLS), lambda a, b: (a // 3) * COLS + a % 3 == b)
    left_put = one_hot(
        (ROWS * 8, 96), lambda a, b: (a % 8 >= 5) & ((a // 8) * 3 + a % 8 - 5 == b)
    )
    right_put = one_hot((ROWS * 8, 96), lambda a, b: (a % 8 < 3) & ((a // 8) * 3 + a % 8 == b))

    def send_columns(n, cells):
        csend[n, 0] = dot(east_pick, cells).astype(BF16)
        csend[n, 1] = dot(west_pick, cells).astype(BF16)
        copies = [
            pltpu.make_async_remote_copy(
                src_ref=csend.at[n, i],
                dst_ref=crecv.at[n, i],
                send_sem=col_s.at[n, i],
                recv_sem=col_r.at[n, i],
                device_id=target,
                device_id_type=MESH,
            )
            for i, target in ((0, east), (1, west))
        ]
        for copy in copies:
            copy.start()
        return copies

    def take_columns(n, copies, field):
        for copy in copies:
            copy.wait()
        field[3 : 3 + ROWS, 0:8, :] = dot(left_put, crecv[n, 0]).reshape(ROWS, 8, C)
        field[3 : 3 + ROWS, 24:32, :] = dot(right_put, crecv[n, 1]).reshape(ROWS, 8, C)

    def send_rows(n, field):
        rsend[n, 0] = field[3:6].astype(BF16)
        rsend[n, 1] = field[ROWS : ROWS + 3].astype(BF16)
        slot = jnp.where(is_top, 0, 1)
        up = pltpu.make_async_remote_copy(
            src_ref=rsend.at[n, 1],
            dst_ref=rrecv.at[n, slot],
            send_sem=row_s.at[n, 1],
            recv_sem=row_r.at[n, slot],
            device_id=north,
            device_id_type=MESH,
        )
        up.start()
        down = pltpu.make_async_remote_copy(
            src_ref=rsend.at[n, 0],
            dst_ref=rrecv.at[n, 0],
            send_sem=row_s.at[n, 0],
            recv_sem=row_r.at[n, 0],
            device_id=south,
            device_id_type=MESH,
        )

        @pl.when(has_south)
        def _():
            down.start()

        return up, down

    def take_rows(n, copies, field):
        up, down = copies
        up.wait_send()
        down.wait_recv()

        @pl.when(has_south)
        def _():
            down.wait_send()
            pltpu.make_async_remote_copy(
                src_ref=rsend.at[n, 1],
                dst_ref=rrecv.at[n, 1],
                send_sem=row_s.at[n, 1],
                recv_sem=row_r.at[n, 1],
                device_id=south,
                device_id_type=MESH,
            ).wait_recv()
            field[0:3] = rrecv[n, 1].astype(F32)

        @pl.when(jnp.logical_not(has_south))
        def _():
            field[0:3] = jnp.zeros((3, WIDE, C), F32)

        @pl.when(is_top)
        def _():
            turn = one_hot((WIDE, WIDE), lambda a, b: a + b == WIDE - 1)
            for m in range(3):
                field[ROWS + 3 + m] = dot(turn, rrecv[n, 0, 2 - m])

        @pl.when(jnp.logical_not(is_top))
        def _():
            field[ROWS + 3 : ROWS + 6] = rrecv[n, 0].astype(F32)

    def shift(field, out):
        @pl.loop(0, PADR)
        def _(r):
            for b in range(7):
                out[b, r] = field[r, 5 + b : 21 + b, :].reshape(2, 8, C)

    def conv_rows(source, r0, rows, flip):
        acc = jnp.zeros((rows, 2, 8, C), F32)
        for b in range(7):
            for a in range(7):
                k = taps[48 - a * 7 - b] if flip else taps[a * 7 + b]
                acc = acc + source[b, pl.ds(r0 + a, rows)] * k
        return acc

    pl.semaphore_wait(
        barrier, 4 + (nplane - 1) + (nz - 1) + jnp.where(has_south, 1, 0)
    )
    own_cells = own.astype(BF16).reshape(CELLS, C)
    copies = send_columns(0, own_cells)
    take_columns(0, copies, pad)
    copies = send_rows(0, pad)
    take_rows(0, copies, pad)
    shift(pad, shifted)

    block = 8
    cells = block * COLS

    @pl.loop(0, ROWS // block)
    def _(blk):
        r0 = blk * block
        here = pl.ds(pl.multiple_of(r0 * COLS, cells), cells)
        mixed = jnp.concatenate(
            [conv_rows(shifted, r0 + 4 * i, 4, False).reshape(4 * COLS, C) for i in range(block // 4)],
            axis=0,
        )
        average = jnp.sum(mixed, axis=1, keepdims=True) * (1.0 / C)
        centred = mixed - average
        variance = jnp.sum(centred * centred, axis=1, keepdims=True) * (1.0 / C)
        inv_std = lax.rsqrt(variance + EPSILON)
        unit = centred * inv_std
        normed = (unit * gain[...] + nbias[...]).astype(BF16)
        normed_s[here, :] = normed
        pre = dot(normed, w_in[...]) + b_hid[...]
        square = pre * pre
        t = jnp.tanh(GELU_A * pre * (1.0 + GELU_B * square))
        half = 0.5 * (1.0 + t)
        hidden = (pre * half).astype(BF16)
        hidden_s[here, :] = hidden
        slope = half + pre * (0.5 * GELU_A) * (1.0 - t * t) * (1.0 + 3.0 * GELU_B * square)
        branch = dot(hidden, w_out[...], ((1,), (1,))) + b_out[...]
        rows_here = pl.ds(r0, block)
        sea_w = maskb[rows_here].reshape(cells, C)
        st = state[rows_here].astype(F32).reshape(cells, C)
        ct = cot[rows_here].astype(F32).reshape(cells, C) * sea_w
        block_out[rows_here] = (
            (sea_w * (st + scale[...] * branch)).astype(BF16).reshape(block, COLS, C)
        )
        grad_branch = ct * scale[...]
        bcot = grad_branch.astype(BF16)
        bcot_s[here, :] = bcot
        grad_pre = dot(bcot, w_out[...]) * slope
        precot = grad_pre.astype(BF16)
        precot_s[here, :] = precot
        grad_normed = dot(precot, w_in[...], ((1,), (1,)))
        grad_unit = grad_normed * gain[...]
        mean_a = jnp.sum(grad_unit, axis=1, keepdims=True) * (1.0 / C)
        mean_b = jnp.sum(grad_unit * unit, axis=1, keepdims=True) * (1.0 / C)
        grad_mixed = inv_std * (grad_unit - mean_a - unit * mean_b)
        mcot = grad_mixed.astype(BF16)
        mcot_s[here, :] = mcot
        padq[pl.ds(3 + r0, block), 8:24, :] = mcot.astype(F32).reshape(block, COLS, C)

        def fold8(v):
            return jnp.sum(v.reshape(cells // 8, 8, v.shape[1]), axis=0)

        sums[0] += fold8(grad_normed * unit)
        sums[1] += fold8(grad_normed)
        sums[2] += fold8(grad_branch)
        sums[3] += fold8(ct * branch)
        sumh[...] += fold8(grad_pre)

    copies = send_columns(1, mcot_s[...])

    for t in range(HID // 256):
        wide = slice(256 * t, 256 * t + 256)
        g_in = dot(normed_s[...], precot_s[:, wide], ((0,), (0,)))
        g_out = dot(bcot_s[...], hidden_s[:, wide], ((0,), (0,)))
        for j in range(2):
            to = slice((2 * t + j) * C, (2 * t + j + 1) * C)
            wbuf[0, to, :] = g_in[:, 128 * j : 128 * j + 128]
            wbuf[1, to, :] = g_out[:, 128 * j : 128 * j + 128]

    def to_pair(i, rows):
        return pltpu.make_async_remote_copy(
            src_ref=wbuf.at[1 - core, rows],
            dst_ref=wrecv.at[rows],
            send_sem=core_s.at[i],
            recv_sem=core_r.at[i],
            device_id=pair,
            device_id_type=MESH,
        )

    pair_w = to_pair(0, pl.ds(0, WROWS))
    pair_w.start()

    take_columns(1, copies, padq)
    copies = send_rows(1, padq)

    for b in range(7):

        def step(i, accs, b=b):
            r0 = i * 4
            m = padq[pl.ds(3 + r0, 4), 8:24, :].reshape(4, 2, 8, C)
            return tuple(
                accs[a] + jnp.sum((m * shifted[b, pl.ds(r0 + a, 4)]).reshape(8, 8, C), axis=0)
                for a in range(7)
            )

        accs = lax.fori_loop(0, ROWS // 4, step, tuple(jnp.zeros((8, C), F32) for _ in range(7)))
        for a in range(7):
            small[a * 7 + b : a * 7 + b + 1, 0:C] = jnp.sum(accs[a], axis=0, keepdims=True)
    for i in range(4):
        small[49 + i : 50 + i, 0:C] = jnp.sum(sums[i], axis=0, keepdims=True)
    hid_row = jnp.sum(sumh[...], axis=0, keepdims=True)
    for i in range(3):
        small[53 + i : 54 + i, :] = hid_row[:, 256 * i : 256 * i + 256]
    wbuf[0, WROWS:, :] = small[:, 0:128]
    wbuf[1, WROWS:, :] = small[:, 128:256]
    pair_s = to_pair(1, pl.ds(WROWS, SROWS))
    pair_s.start()

    take_rows(1, copies, padq)
    pair_w.wait()
    pair_s.wait()

    @pl.loop(0, WROWS // 64)
    def _(i):
        rows = pl.ds(pl.multiple_of(i * 64, 64), 64)
        both = wbuf[core, rows, :] + wrecv[rows, :]
        psum[rows, :] = both
        pay[rows, :] = both.astype(BF16)

    both = wbuf[core, WROWS:, :] + wrecv[WROWS:, :]
    high = both.astype(BF16)
    low = both - high.astype(F32)
    psum[WROWS : WROWS + SROWS, :] = high.astype(F32)
    psum[WROWS + SROWS :, :] = low
    pay[WROWS : WROWS + SROWS, :] = high
    pay[WROWS + SROWS :, :] = low.astype(BF16)

    def rows_of(k, size):
        return pl.ds(pl.multiple_of(k * size, 8), size)

    def plane_copy(k, sender):
        return pltpu.make_async_remote_copy(
            src_ref=pay.at[rows_of(k, chunk)],
            dst_ref=xrecv.at[sender],
            send_sem=xs.at[k],
            recv_sem=xr.at[sender],
            device_id=in_plane(k),
            device_id_type=MESH,
        )

    @pl.loop(1, nplane)
    def _(d):
        plane_copy((plane + d) % nplane, plane).start()

    shift(padq, shiftq)

    @pl.loop(0, ROWS // 4)
    def _(i):
        rows_here = pl.ds(i * 4, 4)
        grad = conv_rows(shiftq, i * 4, 4, True).reshape(4, COLS, C)
        grad_state[rows_here] = (
            maskb[rows_here] * (cot[rows_here].astype(F32) + grad)
        ).astype(BF16)

    @pl.when(is_top)
    def _():
        first = ROWS - 4
        acc = conv_rows(shiftq, first, 4, True)
        parts = [acc[i] for i in range(4)]
        for i in range(1, 4):
            for a in range(7 - i, 7):
                for b in range(7):
                    change = taps[a * 7 + b] - taps[48 - a * 7 - b]
                    parts[i] = parts[i] + shiftq[b, first + i + a] * change
        for i in range(1, 4):
            grad_state[first + i] = (
                maskb[first + i] * (cot[first + i].astype(F32) + parts[i].reshape(COLS, C))
            ).astype(BF16)

    zacc[...] = psum[rows_of(plane, chunk), :]

    @pl.loop(1, nplane)
    def _(d):
        k = (plane + d) % nplane
        copy = plane_copy(k, k)
        copy.wait()
        zacc[...] += xrecv[k].astype(F32)

    def z_copy(k, sender):
        return pltpu.make_async_remote_copy(
            src_ref=zacc.at[rows_of(k, zrows)],
            dst_ref=zrecv.at[sender],
            send_sem=zs.at[k],
            recv_sem=zr.at[sender],
            device_id=in_z(k),
            device_id_type=MESH,
        )

    def z_back(owner, k):
        return pltpu.make_async_remote_copy(
            src_ref=ztot.at[rows_of(owner, zrows)],
            dst_ref=ztot.at[rows_of(owner, zrows)],
            send_sem=zas.at[k],
            recv_sem=zar.at[owner],
            device_id=in_z(k),
            device_id_type=MESH,
        )

    @pl.loop(1, nz)
    def _(d):
        k = (zi + d) % nz

        @pl.when(k < owners)
        def _():
            z_copy(k, zi).start()

    @pl.when(zi < owners)
    def _():
        mine = rows_of(zi, zrows)
        ztot[mine, :] = zacc[mine, :]

        @pl.loop(1, nz)
        def _(d):
            k = (zi + d) % nz
            z_copy(zi, k).wait_recv()
            ztot[mine, :] += zrecv[k]

        @pl.loop(1, nz)
        def _(d):
            z_back(zi, (zi + d) % nz).start()

    @pl.loop(1, nz)
    def _(d):
        k = (zi + d) % nz

        @pl.when(k < owners)
        def _():
            z_copy(k, zi).wait_send()
            z_back(k, k).wait_recv()

    def plane_back(owner, k):
        return pltpu.make_async_remote_copy(
            src_ref=abuf.at[rows_of(owner, chunk)],
            dst_ref=abuf.at[rows_of(owner, chunk)],
            send_sem=xas.at[k],
            recv_sem=xar.at[owner],
            device_id=in_plane(k),
            device_id_type=MESH,
        )

    abuf[rows_of(plane, chunk), :] = ztot[...].astype(BF16)

    @pl.loop(1, nplane)
    def _(d):
        plane_back(plane, (plane + d) % nplane).start()

    @pl.when(zi < owners)
    def _():
        @pl.loop(1, nz)
        def _(d):
            z_back(zi, (zi + d) % nz).wait_send()

    @pl.loop(1, nplane)
    def _(d):
        k = (plane + d) % nplane
        plane_back(k, k).wait()

    last = pltpu.make_async_remote_copy(
        src_ref=abuf,
        dst_ref=fin,
        send_sem=core_s.at[2],
        recv_sem=core_r.at[2],
        device_id=pair,
        device_id_type=MESH,
    )
    last.start()
    total[core] = abuf[...]
    last.wait()
    total[1 - core] = fin[...]


def finish_kernel(factor, total, block, grad, block_out, grad_out, gk, gg, gb, gw_in, gbh, gw_out, gbo, gls):
    block_out[...] = block[...]
    grad_out[...] = grad[...]
    for t in range(HID // 128):
        rows = slice(t * C, (t + 1) * C)
        wide = slice(128 * t, 128 * t + 128)
        gw_in[:, wide] = total[0, rows, :].astype(F32) * factor
        gw_out[:, wide] = total[1, rows, :].astype(F32) * factor
    hi, lo = slice(WROWS, WROWS + SROWS), slice(WROWS + SROWS, TOT)
    left = (total[0, hi, :].astype(F32) + total[0, lo, :].astype(F32)) * factor
    right = (total[1, hi, :].astype(F32) + total[1, lo, :].astype(F32)) * factor
    for a in range(7):
        gk[a, :, 0:128] = left[7 * a : 7 * a + 7]
        gk[a, :, 128:C] = right[7 * a : 7 * a + 7, 0 : C - 128]
    for i, out in enumerate((gg, gb, gbo, gls)):
        out[:, 0:128] = left[49 + i : 50 + i]
        out[:, 128:C] = right[49 + i : 50 + i, 0 : C - 128]
    for i in range(3):
        gbh[:, 256 * i : 256 * i + 128] = left[53 + i : 54 + i]
        gbh[:, 256 * i + 128 : 256 * i + 256] = right[53 + i : 54 + i]


def on_device(
    nlon,
    nlat,
    state,
    land_mask,
    cotangent,
    kernel,
    norm_gain,
    norm_bias,
    weight_in,
    bias_hidden,
    weight_out,
    bias_out,
    layer_scale,
):
    px, nzl, nzh, py = groups(nlon, nlat)
    nplane, nz = px * py, nzl * nzh
    chunk = TOT // nplane
    zrows = max(8, -(-chunk // nz // 8) * 8)
    if zrows * nz < chunk:
        zrows += 8
    vmem = pl.BlockSpec(memory_space=pltpu.VMEM)
    dma = pltpu.SemaphoreType.DMA
    row = lambda v: v.reshape(1, -1)
    block, grad, total = pl.pallas_call(
        functools.partial(main_kernel, nlon, nlat),
        out_shape=(
            jax.ShapeDtypeStruct((ROWS, COLS, C), BF16),
            jax.ShapeDtypeStruct((ROWS, COLS, C), BF16),
            jax.ShapeDtypeStruct((2, TOT, 128), BF16),
        ),
        in_specs=[vmem] * 11,
        out_specs=(vmem,) * 3,
        scratch_shapes=[
            pltpu.VMEM((PADR, WIDE, C), F32),
            pltpu.VMEM((7, PADR, 2, 8, C), F32),
            pltpu.VMEM((PADR, WIDE, C), F32),
            pltpu.VMEM((7, PADR, 2, 8, C), F32),
            pltpu.VMEM((49, 8, C), F32),
            pltpu.VMEM((ROWS, COLS, C), F32),
            pltpu.VMEM((CELLS, C), BF16),
            pltpu.VMEM((CELLS, HID), BF16),
            pltpu.VMEM((CELLS, HID), BF16),
            pltpu.VMEM((CELLS, C), BF16),
            pltpu.VMEM((CELLS, C), BF16),
            pltpu.VMEM((4, 8, C), F32),
            pltpu.VMEM((8, HID), F32),
            pltpu.VMEM((SROWS, 256), F32),
            pltpu.VMEM((2, 2, 96, C), BF16),
            pltpu.VMEM((2, 2, 96, C), BF16),
            pltpu.VMEM((2, 2, 3, WIDE, C), BF16),
            pltpu.VMEM((2, 2, 3, WIDE, C), BF16),
            pltpu.VMEM((2, WROWS + SROWS, 128), F32),
            pltpu.VMEM((WROWS + SROWS, 128), F32),
            pltpu.VMEM((TOT, 128), F32),
            pltpu.VMEM((TOT, 128), BF16),
            pltpu.VMEM((nplane, chunk, 128), BF16),
            pltpu.VMEM((chunk, 128), F32),
            pltpu.VMEM((nz, zrows, 128), F32),
            pltpu.VMEM((chunk, 128), F32),
            pltpu.VMEM((TOT, 128), BF16),
            pltpu.VMEM((TOT, 128), BF16),
            dma((2, 2)),
            dma((2, 2)),
            dma((2, 2)),
            dma((2, 2)),
            dma((3,)),
            dma((3,)),
            dma((nplane,)),
            dma((nplane,)),
            dma((nz,)),
            dma((nz,)),
            dma((nz,)),
            dma((nz,)),
            dma((nplane,)),
            dma((nplane,)),
        ],
        compiler_params=pltpu.CompilerParams(
            collective_id=0, has_side_effects=True, vmem_limit_bytes=48 * 1024 * 1024
        ),
        name="block",
    )(
        state,
        land_mask.T,
        cotangent,
        kernel,
        row(norm_gain),
        row(norm_bias),
        weight_in,
        row(bias_hidden),
        weight_out.T,
        row(bias_out),
        row(layer_scale),
    )
    factor = 1.0 / math.sqrt(ROWS * nlat * COLS * nlon)
    shape = lambda *s: jax.ShapeDtypeStruct(s, F32)
    outs = pl.pallas_call(
        functools.partial(finish_kernel, factor),
        out_shape=(
            jax.ShapeDtypeStruct((ROWS, COLS, C), BF16),
            jax.ShapeDtypeStruct((ROWS, COLS, C), BF16),
            shape(7, 7, C),
            shape(1, C),
            shape(1, C),
            shape(C, HID),
            shape(1, HID),
            shape(C, HID),
            shape(1, C),
            shape(1, C),
        ),
        in_specs=[vmem] * 3,
        out_specs=(vmem,) * 10,
        compiler_params=pltpu.CompilerParams(vmem_limit_bytes=32 * 1024 * 1024),
        name="finish",
    )(total, block, grad)
    outs = [o.reshape(-1) if o.shape[0] == 1 else o for o in outs]
    outs[7] = outs[7].T
    return tuple(outs)


def solution(mesh):
    cells, plane, whole = P("lat", "lon", None), P("lat", "lon"), P()
    return jax.shard_map(
        functools.partial(on_device, mesh.shape["lon"], mesh.shape["lat"]),
        mesh=mesh,
        in_specs=(cells, plane, cells) + (whole,) * 8,
        out_specs=(cells, cells) + (whole,) * 8,
        check_vma=False,
    )
```

time: 629 us -> 102 us (0.16)
  waiting for transfers between devices: 347 us -> 0 us
  blocking collectives: 114 us -> 0 us
  starting transfers between devices: 103 us -> 0 us
  Pallas kernels: 0 us -> 94.4 us
  other arithmetic: 29.1 us -> 0.61 us
  between operations: 15.8 us -> 0.7 us
  matrix products: 9.39 us -> 0 us
    psum x1 -> x0, waiting for transfers between devices: 325 us -> none  [on_device(): lax.psum((partials[0], partials[1], partials[2], partials[3], partials[4]...]
    psum x1 -> x0, blocking collectives: 114 us -> none  [on_device(): lax.psum((partials[0], partials[1], partials[2], partials[3], partials[4]...]
    ppermute x20 -> x0, starting transfers between devices: 103 us -> none  [the longest x12 55.5 us: from_partner(): return lax.ppermute(value, axis, pairs)]
    pallas_call x0 -> x2, Pallas kernels: none -> 94.4 us  [the longest x1 93.2 us: on_device(): pl.pallas_call(functools.partial(main_kernel, nlon, nlat), out_shape=(jax...]
    ppermute x20 -> x0, waiting for transfers between devices: 21.9 us -> none  [the longest x12 19.4 us: from_partner(): return lax.ppermute(value, axis, pairs)]
    reduce_sum x7 -> x0, other arithmetic: 11.7 us -> none  [the longest x1 5.12 us: cell_pass(): average = jnp.mean(mixed, axis=2, keepdims=True)]
    dot_general x6 -> x0, matrix products: 9.39 us -> none  [the longest x2 3.54 us: outer_sum(): lax.dot_general(left, right, (((0,), (0,)), ((), ())), preferred_element_...]
    mul x13 -> x0, other arithmetic: 8.22 us -> none  [the longest x8 6.31 us: on_device(): scaled = tuple((part * factor for part in summed))]
  transfers between devices with their start and end apart: 21 -> 0, of which waited for: 12 -> 0; matrix products, arithmetic and copies ran while one was open for 4% -> 0% of each run, Pallas kernels for 0% -> 0%
where the time goes in v1:
time: 102 us
  Pallas kernels  94.4 us (93%)
  local copies, waits for them, and re-layouts  5.94 us (6%)
    pallas_call x1, Pallas kernels, on_device(): pl.pallas_call(functools.partial(main_kernel, nlon, nlat), out_shape=(jax...  93.2 us
    unnamed x22, local copies, waits for them, and re-layouts  5.94 us

profile of v1, /device:TPU:1, one launch (start us, length us, event | category | flops | bytes accessed | tf_op | source)
XLA Modules:
  0.0 101.7 jit_solution(284403802326106653)
XLA Ops:
  0.6 0.0 copy-start.10
  0.7 0.0 copy-start.5
  0.7 0.7 copy-done.10
  1.3 0.0 copy-start.6
  1.3 0.0 copy-start.7
  1.3 0.0 copy-start.8
  1.3 0.0 copy-start.9
  1.4 0.0 copy-done.5
  1.4 0.6 copy-done.6
  2.0 0.0 copy-done.7
  2.0 0.0 copy-done.8
  2.0 0.0 copy-done.9
  2.1 0.0 copy-start
  2.1 1.0 copy-done
  3.0 0.0 copy-start.1
  3.0 1.0 copy-done.1
  4.0 0.0 copy-start.2
  4.0 0.9 copy-done.2
  4.9 0.0 copy-start.3
  4.9 0.9 copy-done.3
  5.9 0.0 copy-start.4
  5.9 0.7 copy-done.4
  6.6 93.2 %block.1 = (bf16[32,16,192]{2,1,0:T(8,128)(2,1)S(1)}, bf16[32,16,192]{2,1,0:T(8,128)(2,1)S(1)}, bf16[2,1280,128]{2,1,0:T(8,128)(2,1)S(1)}) custom-call(bf16[32,16,192]{2,1,0:T(8,128)(2,1)S(1)} %copy-done.2, s32[16,32]{1,0:T(8,128)S(1)} %bitcast.12, bf16[32,16,192]{2,1,0:T(8,128)(2,1)S(1)} %copy-done.3, bf16[7,7,192]{2,1,0:T(8,128)(2,1)S(1)} %copy-done.4, ...), custom_call_target="tpu_custom_call" | custom-call | tf_op jit(solution)/shard_map/block/pallas_call | solution.py:607
  99.8 1.3 %finish.1 = (bf16[32,16,192]{2,1,0:T(8,128)(2,1)}, bf16[32,16,192]{2,1,0:T(8,128)(2,1)}, f32[7,7,192]{2,1,0:T(8,128)}, f32[1,192]{1,0:T(1,128)}, f32[1,192]{1,0:...) custom-call(bf16[2,1280,128]{2,1,0:T(8,128)(2,1)S(1)} %get-tuple-ele, ...), custom_call_target="tpu_custom_call" | custom-call | tf_op jit(solution)/shard_map/finish/pallas_call | solution.py:679
  101.1 0.6 reduce
  (1 shorter events, 0.0 us)
Async XLA Ops:
  0.6 0.7 copy-start.10
  0.7 0.7 copy-start.5
  1.3 0.7 copy-start.6
  1.3 0.7 copy-start.7
  1.3 0.7 copy-start.8
  1.3 0.7 copy-start.9
  2.1 1.0 copy-start
  3.0 1.0 copy-start.1
  4.0 0.9 copy-start.2
  4.9 0.9 copy-start.3
  5.9 0.7 copy-start.4

commit v2 on v1

v2 whole, which is shorter than its diff:
```python
import functools
import math

import jax
import jax.numpy as jnp
from jax import lax
from jax.experimental import pallas as pl
from jax.experimental.pallas import tpu as pltpu
from jax.sharding import PartitionSpec as P

EPSILON = 1e-06
MESH = pl.DeviceIdType.MESH
F32 = jnp.float32
BF16 = jnp.bfloat16

ROWS, COLS, C, HID = 32, 16, 192, 768
CELLS = ROWS * COLS
PADR, WIDE = ROWS + 6, 32
WROWS = C * HID // 128
SROWS = 64
TOT = WROWS + 2 * SROWS
MAIN = 1024
GELU_A = math.sqrt(2.0 / math.pi)
GELU_B = 0.044715


def groups(nlon, nlat):
    px = 4 if nlon >= 64 else 1
    nzl = nlon // (2 * px)
    nzh = 2 if nlat >= 8 else 1
    return px, nzl, nzh, nlat // nzh


def shares(nlon, nlat):
    px, nzl, nzh, py = groups(nlon, nlat)
    size = px * py * 2
    return size, nzl * nzh // 2, MAIN // size, max(16, (TOT - MAIN) // size)


def one_hot(shape, pick):
    a = lax.broadcasted_iota(jnp.int32, shape, 0)
    b = lax.broadcasted_iota(jnp.int32, shape, 1)
    return pick(a, b).astype(F32).astype(BF16)


def dot(a, b, contract=((1,), (0,))):
    return lax.dot_general(a, b, (contract, ((), ())), preferred_element_type=F32)


def remote(kind, src, dst, send, recv, target):
    return pltpu.make_async_remote_copy(
        src_ref=src,
        dst_ref=dst,
        send_sem=send,
        recv_sem=recv,
        device_id=target,
        device_id_type=MESH,
    )


def main_kernel(
    nlon,
    nlat,
    state_h,
    mask_h,
    cot_h,
    kern_h,
    gain_h,
    nbias_h,
    w_in_h,
    b_hid_h,
    w_out_h,
    b_out_h,
    scale_h,
    block_h,
    grad_h,
    total,
    block_out,
    grad_state,
    state,
    mask,
    cot,
    kern,
    gain,
    nbias,
    w_in,
    b_hid,
    w_out,
    b_out,
    scale,
    pad,
    shifted,
    padq,
    shiftq,
    taps,
    maskb,
    normed_s,
    precot_s,
    hidden_s,
    bcot_s,
    own_s,
    sums,
    sumh,
    small,
    csend,
    ksend,
    crecv,
    vrecv,
    wbuf,
    wrecv,
    psum,
    extra,
    pay,
    xrecv,
    zslot,
    abuf,
    fin,
    load_s,
    store_s,
    halo_s,
    halo_r,
    core_s,
    core_r,
    xs,
    xr,
    zs,
    zr,
    xas,
    xar,
):
    px, nzl, nzh, py = groups(nlon, nlat)
    size, nz, mrows, erows = shares(nlon, nlat)

    loads = [
        pltpu.make_async_copy(src, dst, load_s.at[i])
        for i, (src, dst) in enumerate(
            (
                (state_h, state),
                (mask_h, mask),
                (kern_h, kern),
                (cot_h, cot),
                (w_in_h, w_in),
                (w_out_h, w_out),
                (gain_h, gain),
                (nbias_h, nbias),
                (b_hid_h, b_hid),
                (b_out_h, b_out),
                (scale_h, scale),
            )
        )
    ]
    for load in loads[:3]:
        load.start()

    lon = lax.axis_index("lon")
    lat = lax.axis_index("lat")
    core = lax.rem(lon, 2)
    x = lax.rem(lax.div(lon, 2), px)
    zl = lax.div(lon, 2 * px)
    zh = lax.rem(lat, nzh)
    y = lax.div(lat, nzh)
    odd = lax.rem(zl, 2)
    me = (y * px + x) * 2 + odd
    zi = zh * (nzl // 2) + lax.div(zl, 2)
    is_top = lat == nlat - 1
    has_south = lat > 0

    def device(la, lo):
        return {"lon": lo, "lat": la}

    right, left = lax.rem(lon + 1, nlon), lax.rem(lon + nlon - 1, nlon)
    above, below = jnp.where(is_top, lat, lat + 1), jnp.where(has_south, lat - 1, 0)
    fold_r, fold_l = lax.rem(2 * nlon - 2 - lon, nlon), lax.rem(nlon - lon, nlon)
    east, west = device(lat, right), device(lat, left)
    north = device(above, jnp.where(is_top, nlon - 1 - lon, lon))
    south = device(below, lon)
    top_r = device(above, jnp.where(is_top, fold_r, right))
    top_l = device(above, jnp.where(is_top, fold_l, left))
    bot_r, bot_l = device(below, right), device(below, left)
    self_r = jnp.logical_and(is_top, fold_r == lon)
    self_l = jnp.logical_and(is_top, fold_l == lon)
    other_r, other_l = jnp.logical_not(self_r), jnp.logical_not(self_l)
    pair = device(lat, lon + 1 - 2 * core)

    def in_group(k):
        p = lax.div(k, 2)
        z = zl - odd + lax.rem(k, 2)
        return device(lax.div(p, px) * nzh + zh, z * (2 * px) + lax.rem(p, px) * 2 + core)

    def in_z(k):
        z = lax.rem(k, nzl // 2) * 2 + odd
        return device(y * nzh + lax.div(k, nzl // 2), z * (2 * px) + x * 2 + core)

    def shift(field, out):
        @pl.loop(0, PADR)
        def _(r):
            for b in range(7):
                out[b, r] = field[r, 5 + b : 21 + b, :].reshape(2, 8, C)

    def conv_rows(source, r0, rows, flip):
        acc = jnp.zeros((rows, 2, 8, C), F32)
        for b in range(7):
            for a in range(7):
                k = taps[48 - a * 7 - b] if flip else taps[a * 7 + b]
                acc = acc + source[b, pl.ds(r0 + a, rows)] * k
        return acc

    barrier = pltpu.get_barrier_semaphore()

    def hello(target):
        pl.semaphore_signal(barrier, inc=1, device_id=target, device_id_type=MESH)

    hello(north)

    @pl.when(has_south)
    def _():
        hello(south)
        hello(bot_r)
        hello(bot_l)

    @pl.when(other_r)
    def _():
        hello(top_r)

    @pl.when(other_l)
    def _():
        hello(top_l)

    hello(east)
    hello(west)

    @pl.loop(1, nz)
    def _(d):
        hello(in_z(lax.rem(zi + d, nz)))

    @pl.loop(1, size)
    def _(d):
        hello(in_group(lax.rem(me + d, size)))

    hello(pair)
    for load in loads[3:]:
        load.start()

    by_row = one_hot((CELLS, ROWS), lambda a, b: a // COLS == b)
    by_col = one_hot((CELLS, COLS), lambda a, b: a % COLS == b).astype(F32)

    def pick_cell(a):
        e = (a // 3) * COLS + 13 + a % 3
        w = ((a - 96) // 3) * COLS + (a - 96) % 3
        c, i = (a - 192) // 16, (a - 192) % 16
        corner = (i // 3 + (ROWS - 3) * (c // 2)) * COLS + i % 3 + 13 * (c % 2)
        return jnp.where(a < 96, e, jnp.where(a < 192, w, jnp.where(i < 9, corner, -1)))

    picks = one_hot((256, CELLS), lambda a, b: pick_cell(a) == b)
    left_put = one_hot(
        (ROWS * 8, 96), lambda a, b: (a % 8 >= 5) & ((a // 8) * 3 + a % 8 - 5 == b)
    )
    right_put = one_hot((ROWS * 8, 96), lambda a, b: (a % 8 < 3) & ((a // 8) * 3 + a % 8 == b))

    def put_cell(a, fold):
        m, q = a // WIDE, a % WIDE
        row = jnp.where(fold, 2 - m, m)
        mid = row * COLS + jnp.where(fold, 23 - q, q - 8)
        lo = 48 + row * 3 + jnp.where(fold, 7 - q, q - 5)
        hi = 64 + row * 3 + jnp.where(fold, 26 - q, q - 24)
        hi = jnp.where((q >= 24) & (q < 27), hi, -1)
        return jnp.where((q >= 8) & (q < 24), mid, jnp.where((q >= 5) & (q < 8), lo, hi))

    north_put = one_hot((3 * WIDE, 80), lambda a, b: put_cell(a, is_top) == b)
    south_put = one_hot((3 * WIDE, 80), lambda a, b: put_cell(a, False) == b)

    def halo_copies(n):
        slot = jnp.where(is_top, 0, 1)

        def copy(src, dst, s, r, target):
            return remote("halo", src, dst, halo_s.at[n, s], halo_r.at[n, r], target)

        corner = ksend.at[n]
        return dict(
            e=copy(csend.at[n, 0], crecv.at[n, 0], 0, 0, east),
            w=copy(csend.at[n, 1], crecv.at[n, 1], 1, 1, west),
            up=copy(own_s.at[n, ROWS - 3 : ROWS], vrecv.at[n, slot, 0:3], 2, 2 + slot, north),
            tr=copy(
                corner.at[3],
                vrecv.at[n, slot, 4 - slot],
                3,
                jnp.where(is_top, 5, 6),
                top_r,
            ),
            tl=copy(
                corner.at[2],
                vrecv.at[n, slot, 3 + slot],
                4,
                jnp.where(is_top, 4, 7),
                top_l,
            ),
            down=copy(own_s.at[n, 0:3], vrecv.at[n, 0, 0:3], 5, 2, south),
            br=copy(corner.at[1], vrecv.at[n, 0, 3], 6, 4, bot_r),
            bl=copy(corner.at[0], vrecv.at[n, 0, 4], 7, 5, bot_l),
        )

    def pick_halo(n):
        picked = dot(picks, own_s[n].reshape(CELLS, C)).astype(BF16)
        csend[n] = picked[0:192].reshape(2, 96, C)
        ksend[n] = picked[192:256].reshape(4, 16, C)

    def send_halo(n):
        copies = halo_copies(n)
        copies["up"].start()

        @pl.when(has_south)
        def _():
            copies["down"].start()
            copies["br"].start()
            copies["bl"].start()

        @pl.when(other_r)
        def _():
            copies["tr"].start()

        @pl.when(other_l)
        def _():
            copies["tl"].start()

        copies["e"].start()
        copies["w"].start()

        @pl.when(self_r)
        def _():
            vrecv[n, 0, 4] = ksend[n, 3]

        @pl.when(self_l)
        def _():
            vrecv[n, 0, 3] = ksend[n, 2]

    def take_halo(n, field):
        copies = halo_copies(n)

        def arrive(piece, r):
            remote("halo", piece, piece, halo_s.at[n, 0], halo_r.at[n, r], east).wait_recv()

        copies["e"].wait()
        copies["w"].wait()
        field[3 : 3 + ROWS, 0:8, :] = dot(left_put, crecv[n, 0]).reshape(ROWS, 8, C)
        field[3 : 3 + ROWS, 24:32, :] = dot(right_put, crecv[n, 1]).reshape(ROWS, 8, C)
        copies["up"].wait_send()
        arrive(vrecv.at[n, 0, 0:3], 2)

        @pl.when(other_r)
        def _():
            copies["tr"].wait_send()
            arrive(vrecv.at[n, 0, 4], 5)

        @pl.when(other_l)
        def _():
            copies["tl"].wait_send()
            arrive(vrecv.at[n, 0, 3], 4)

        field[ROWS + 3 : ROWS + 6] = dot(north_put, vrecv[n, 0].reshape(80, C)).reshape(3, WIDE, C)

        @pl.when(has_south)
        def _():
            for name in ("down", "br", "bl"):
                copies[name].wait_send()
            arrive(vrecv.at[n, 1, 0:3], 3)
            arrive(vrecv.at[n, 1, 3], 6)
            arrive(vrecv.at[n, 1, 4], 7)
            field[0:3] = dot(south_put, vrecv[n, 1].reshape(80, C)).reshape(3, WIDE, C)

        @pl.when(jnp.logical_not(has_south))
        def _():
            field[0:3] = jnp.zeros((3, WIDE, C), F32)

    for load in loads[:3]:
        load.wait()
    sea = dot(by_row, mask[...].astype(F32).astype(BF16), ((1,), (1,))) * by_col
    maskb[...] = dot(sea.astype(BF16), jnp.ones((COLS, C), BF16)).reshape(ROWS, COLS, C)
    own = state[...].astype(F32) * maskb[...]
    pad[3 : 3 + ROWS, 8:24, :] = own
    own_s[0] = own.astype(BF16)
    pick_halo(0)
    for a in range(7):
        k7 = kern[a].astype(F32)
        for b in range(7):
            taps[a * 7 + b] = jnp.broadcast_to(k7[b : b + 1], (8, C))
    sums[...] = jnp.zeros_like(sums)
    sumh[...] = jnp.zeros_like(sumh)
    small[...] = jnp.zeros_like(small)
    extra[...] = jnp.zeros_like(extra)

    hellos = 4 + (size - 1) + (nz - 1) + jnp.where(has_south, 3, 0)
    hellos = hellos + jnp.where(other_r, 1, 0) + jnp.where(other_l, 1, 0)
    pl.semaphore_wait(barrier, hellos)
    send_halo(0)
    for load in loads[3:]:
        load.wait()
    take_halo(0, pad)
    shift(pad, shifted)

    block = 8
    cells = block * COLS

    @pl.loop(0, ROWS // block)
    def _(blk):
        r0 = blk * block
        here = pl.ds(pl.multiple_of(r0 * COLS, cells), cells)
        mixed = jnp.concatenate(
            [conv_rows(shifted, r0 + 4 * i, 4, False).reshape(4 * COLS, C) for i in range(block // 4)],
            axis=0,
        )
        average = jnp.sum(mixed, axis=1, keepdims=True) * (1.0 / C)
        centred = mixed - average
        variance = jnp.sum(centred * centred, axis=1, keepdims=True) * (1.0 / C)
        inv_std = lax.rsqrt(variance + EPSILON)
        unit = centred * inv_std
        normed = (unit * gain[...] + nbias[...]).astype(BF16)
        normed_s[here, :] = normed
        pre = dot(normed, w_in[...]) + b_hid[...].reshape(HID)
        square = pre * pre
        t = jnp.tanh(GELU_A * pre * (1.0 + GELU_B * square))
        half = 0.5 * (1.0 + t)
        hidden = (pre * half).astype(BF16)
        hidden_s[here, :] = hidden
        slope = half + pre * (0.5 * GELU_A) * (1.0 - t * t) * (1.0 + 3.0 * GELU_B * square)
        branch = dot(hidden, w_out[...], ((1,), (1,))) + b_out[...]
        rows_here = pl.ds(r0, block)
        sea_w = maskb[rows_here].reshape(cells, C)
        st = state[rows_here].astype(F32).reshape(cells, C)
        ct = cot[rows_here].astype(F32).reshape(cells, C) * sea_w
        block_out[rows_here] = (
            (sea_w * (st + scale[...] * branch)).astype(BF16).reshape(block, COLS, C)
        )
        grad_branch = ct * scale[...]
        bcot = grad_branch.astype(BF16)
        bcot_s[here, :] = bcot
        grad_pre = dot(bcot, w_out[...]) * slope
        precot = grad_pre.astype(BF16)
        precot_s[here, :] = precot
        grad_normed = dot(precot, w_in[...], ((1,), (1,)))
        grad_unit = grad_normed * gain[...]
        mean_a = jnp.sum(grad_unit, axis=1, keepdims=True) * (1.0 / C)
        mean_b = jnp.sum(grad_unit * unit, axis=1, keepdims=True) * (1.0 / C)
        grad_mixed = inv_std * (grad_unit - mean_a - unit * mean_b)
        mcot = grad_mixed.astype(BF16)
        own_s[1, rows_here] = mcot.reshape(block, COLS, C)
        padq[pl.ds(3 + r0, block), 8:24, :] = mcot.astype(F32).reshape(block, COLS, C)

        def fold8(v):
            return jnp.sum(v.reshape(cells // 8, 8, v.shape[1]), axis=0)

        sums[0] += fold8(grad_normed * unit)
        sums[1] += fold8(grad_normed)
        sums[2] += fold8(grad_branch)
        sums[3] += fold8(ct * branch)
        sumh[...] += fold8(grad_pre)

    pick_halo(1)
    send_halo(1)
    block_store = pltpu.make_async_copy(block_out, block_h, store_s.at[0])
    block_store.start()

    for t in range(HID // 256):
        wide = slice(256 * t, 256 * t + 256)
        g_in = dot(normed_s[...], precot_s[:, wide], ((0,), (0,)))
        g_out = dot(bcot_s[...], hidden_s[:, wide], ((0,), (0,)))
        for j in range(2):
            to = slice((2 * t + j) * C, (2 * t + j + 1) * C)
            wbuf[0, to, :] = g_in[:, 128 * j : 128 * j + 128]
            wbuf[1, to, :] = g_out[:, 128 * j : 128 * j + 128]

    def to_pair(i, rows):
        return remote("pair", wbuf.at[1 - core, rows], wrecv.at[rows], core_s.at[i], core_r.at[i], pair)

    pair_w = to_pair(0, pl.ds(0, WROWS))
    pair_w.start()

    for b in range(7):

        def step(i, accs, b=b):
            r0 = i * 4
            m = padq[pl.ds(3 + r0, 4), 8:24, :].reshape(4, 2, 8, C)
            return tuple(
                accs[a] + jnp.sum((m * shifted[b, pl.ds(r0 + a, 4)]).reshape(8, 8, C), axis=0)
                for a in range(7)
            )

        accs = lax.fori_loop(0, ROWS // 4, step, tuple(jnp.zeros((8, C), F32) for _ in range(7)))
        for a in range(7):
            small[a * 7 + b : a * 7 + b + 1, 0:C] = jnp.sum(accs[a], axis=0, keepdims=True)
    for i in range(4):
        small[49 + i : 50 + i, 0:C] = jnp.sum(sums[i], axis=0, keepdims=True)
    hid_row = jnp.sum(sumh[...], axis=0, keepdims=True)
    for i in range(3):
        small[53 + i : 54 + i, :] = hid_row[:, 256 * i : 256 * i + 256]
    wbuf[0, WROWS:, :] = small[:, 0:128]
    wbuf[1, WROWS:, :] = small[:, 128:256]
    pair_s = to_pair(1, pl.ds(WROWS, SROWS))
    pair_s.start()

    pair_w.wait()

    @pl.loop(0, size)
    def _(k):
        rows = pl.ds(pl.multiple_of(k * mrows, 32), mrows)
        both = wbuf[core, rows, :] + wrecv[rows, :]
        psum[rows, :] = both
        pay[k, 0:mrows, :] = both.astype(BF16)

    pair_s.wait()
    rest_w = wbuf[core, MAIN:WROWS, :] + wrecv[MAIN:WROWS, :]
    both = wbuf[core, WROWS:, :] + wrecv[WROWS:, :]
    high = both.astype(BF16).astype(F32)
    other = jnp.concatenate([rest_w, high, both - high], axis=0)
    for i in range((TOT - MAIN) // size):
        extra[pl.ds(i, size, stride=erows), :] = other[i * size : (i + 1) * size]
    pay[:, mrows:, :] = extra[...].reshape(size, erows, 128).astype(BF16)

    def group_copy(k, sender):
        return remote("group", pay.at[k], xrecv.at[sender], xs.at[k], xr.at[sender], in_group(k))

    @pl.loop(1, size)
    def _(d):
        k = lax.rem(me + d, size)
        group_copy(k, me).start()

    def halves(v):
        first = (WROWS - MAIN) // size
        count = SROWS // size
        end = v.shape[0]
        row = lax.broadcasted_iota(jnp.int32, v.shape, 0) - mrows
        whole = v + pltpu.roll(v, end - count, 0)
        top = whole.astype(BF16).astype(F32)
        low = pltpu.roll(whole - top, count, 0)
        is_high = (row >= first) & (row < first + count)
        is_low = (row >= first + count) & (row < first + 2 * count)
        return jnp.where(is_high, top, jnp.where(is_low, low, v)).astype(BF16)

    @pl.loop(1, size)
    def _(d):
        k = lax.rem(me + d, size)
        group_copy(k, k).wait()

    def add_chunk(d, acc):
        return acc + xrecv[lax.rem(me + d, size)].astype(F32)

    mine = jnp.concatenate(
        [
            psum[pl.ds(pl.multiple_of(me * mrows, 32), mrows), :],
            extra[pl.ds(pl.multiple_of(me * erows, 16), erows), :],
        ],
        axis=0,
    )
    zslot[zi] = halves(lax.fori_loop(1, size, add_chunk, mine))

    def z_copy(k, sender):
        return remote("z", zslot.at[sender], zslot.at[sender], zs.at[k], zr.at[sender], in_z(k))

    @pl.loop(1, nz)
    def _(d):
        z_copy(lax.rem(zi + d, nz), zi).start()

    take_halo(1, padq)
    shift(padq, shiftq)

    @pl.loop(0, ROWS // 4)
    def _(i):
        rows_here = pl.ds(i * 4, 4)
        grad = conv_rows(shiftq, i * 4, 4, True).reshape(4, COLS, C)
        grad_state[rows_here] = (
            maskb[rows_here] * (cot[rows_here].astype(F32) + grad)
        ).astype(BF16)

    @pl.when(is_top)
    def _():
        first = ROWS - 4
        acc = conv_rows(shiftq, first, 4, True)
        parts = [acc[i] for i in range(4)]
        for i in range(1, 4):
            for a in range(7 - i, 7):
                for b in range(7):
                    change = taps[a * 7 + b] - taps[48 - a * 7 - b]
                    parts[i] = parts[i] + shiftq[b, first + i + a] * change
        for i in range(1, 4):
            grad_state[first + i] = (
                maskb[first + i] * (cot[first + i].astype(F32) + parts[i].reshape(COLS, C))
            ).astype(BF16)

    grad_store = pltpu.make_async_copy(grad_state, grad_h, store_s.at[1])
    grad_store.start()

    @pl.loop(1, nz)
    def _(d):
        k = lax.rem(zi + d, nz)
        z_copy(k, k).wait()

    whole = zslot[0].astype(F32)
    for k in range(1, nz):
        whole = whole + zslot[k].astype(F32)
    abuf[me] = halves(whole)

    def back_copy(owner, k):
        return remote("back", abuf.at[owner], abuf.at[owner], xas.at[k], xar.at[owner], in_group(k))

    @pl.loop(1, size)
    def _(d):
        back_copy(me, lax.rem(me + d, size)).start()

    @pl.loop(1, size)
    def _(d):
        k = lax.rem(me + d, size)
        back_copy(k, k).wait()

    last = remote("last", abuf, fin, core_s.at[2], core_r.at[2], pair)
    last.start()
    own_store = pltpu.make_async_copy(abuf, total.at[core], store_s.at[2])
    own_store.start()
    last.wait()
    fin_store = pltpu.make_async_copy(fin, total.at[1 - core], store_s.at[3])
    fin_store.start()
    for store in (block_store, grad_store, own_store, fin_store):
        store.wait()


def finish_kernel(
    factor, size, mrows, erows, total_h, block, grad,
    block_out, grad_out, gk, gg, gb, gw_in, gbh, gw_out, gbo, gls, total, extra, sem,
):
    moves = [
        pltpu.make_async_copy(src, dst, sem.at[i])
        for i, (src, dst) in enumerate(
            ((total_h, total), (block, block_out), (grad, grad_out))
        )
    ]
    for move in moves:
        move.start()
    moves[0].wait()
    small = []
    for c, gw in ((0, gw_in), (1, gw_out)):
        rows = total[c, :, 0:mrows, :].reshape(MAIN, 128).astype(F32) * factor
        extra[...] = total[c, :, mrows:, :].reshape(size * erows, 128).astype(F32) * factor
        rest = [extra[pl.ds(i, size, stride=erows), :] for i in range((TOT - MAIN) // size)]
        rows = jnp.concatenate([rows] + rest, axis=0)
        for t in range(HID // 128):
            gw[:, 128 * t : 128 * t + 128] = rows[t * C : (t + 1) * C]
        small.append(rows[WROWS : WROWS + SROWS] + rows[WROWS + SROWS :])
    near, far = small
    for a in range(7):
        gk[a, :, 0:128] = near[7 * a : 7 * a + 7]
        gk[a, :, 128:C] = far[7 * a : 7 * a + 7, 0 : C - 128]
    for i, out in enumerate((gg, gb, gbo, gls)):
        out[:, 0:128] = near[49 + i : 50 + i]
        out[:, 128:C] = far[49 + i : 50 + i, 0 : C - 128]
    for i in range(3):
        gbh[256 * i : 256 * i + 128] = near[53 + i]
        gbh[256 * i + 128 : 256 * i + 256] = far[53 + i]
    for move in moves[1:]:
        move.wait()


def on_device(
    nlon,
    nlat,
    state,
    land_mask,
    cotangent,
    kernel,
    norm_gain,
    norm_bias,
    weight_in,
    bias_hidden,
    weight_out,
    bias_out,
    layer_scale,
):
    size, nz, mrows, erows = shares(nlon, nlat)
    hbm = pl.BlockSpec(memory_space=pltpu.HBM)
    vmem = pl.BlockSpec(memory_space=pltpu.VMEM)
    dma = pltpu.SemaphoreType.DMA
    row = lambda v: v.reshape(1, -1)
    block, grad, total = pl.pallas_call(
        functools.partial(main_kernel, nlon, nlat),
        out_shape=(
            jax.ShapeDtypeStruct((ROWS, COLS, C), BF16),
            jax.ShapeDtypeStruct((ROWS, COLS, C), BF16),
            jax.ShapeDtypeStruct((2, size, mrows + erows, 128), BF16),
        ),
        in_specs=[hbm] * 11,
        out_specs=(hbm,) * 3,
        scratch_shapes=[
            pltpu.VMEM((ROWS, COLS, C), BF16),
            pltpu.VMEM((ROWS, COLS, C), BF16),
            pltpu.VMEM((ROWS, COLS, C), BF16),
            pltpu.VMEM((COLS, ROWS), jnp.int32),
            pltpu.VMEM((ROWS, COLS, C), BF16),
            pltpu.VMEM((7, 7, C), BF16),
            pltpu.VMEM((1, C), F32),
            pltpu.VMEM((1, C), F32),
            pltpu.VMEM((C, HID), BF16),
            pltpu.VMEM((HID,), F32),
            pltpu.VMEM((C, HID), BF16),
            pltpu.VMEM((1, C), F32),
            pltpu.VMEM((1, C), F32),
            pltpu.VMEM((PADR, WIDE, C), F32),
            pltpu.VMEM((7, PADR, 2, 8, C), F32),
            pltpu.VMEM((PADR, WIDE, C), F32),
            pltpu.VMEM((7, PADR, 2, 8, C), F32),
            pltpu.VMEM((49, 8, C), F32),
            pltpu.VMEM((ROWS, COLS, C), F32),
            pltpu.VMEM((CELLS, C), BF16),
            pltpu.VMEM((CELLS, HID), BF16),
            pltpu.VMEM((CELLS, HID), BF16),
            pltpu.VMEM((CELLS, C), BF16),
            pltpu.VMEM((2, ROWS, COLS, C), BF16),
            pltpu.VMEM((4, 8, C), F32),
            pltpu.VMEM((8, HID), F32),
            pltpu.VMEM((SROWS, 256), F32),
            pltpu.VMEM((2, 2, 96, C), BF16),
            pltpu.VMEM((2, 4, 16, C), BF16),
            pltpu.VMEM((2, 2, 96, C), BF16),
            pltpu.VMEM((2, 2, 5, 16, C), BF16),
            pltpu.VMEM((2, WROWS + SROWS, 128), F32),
            pltpu.VMEM((WROWS + SROWS, 128), F32),
            pltpu.VMEM((MAIN, 128), F32),
            pltpu.VMEM((size * erows, 128), F32),
            pltpu.VMEM((size, mrows + erows, 128), BF16),
            pltpu.VMEM((size, mrows + erows, 128), BF16),
            pltpu.VMEM((nz, mrows + erows, 128), BF16),
            pltpu.VMEM((size, mrows + erows, 128), BF16),
            pltpu.VMEM((size, mrows + erows, 128), BF16),
            dma((11,)),
            dma((4,)),
            dma((2, 8)),
            dma((2, 8)),
            dma((3,)),
            dma((3,)),
            dma((size,)),
            dma((size,)),
            dma((nz,)),
            dma((nz,)),
            dma((size,)),
            dma((size,)),
        ],
        compiler_params=pltpu.CompilerParams(
            collective_id=0, has_side_effects=True, vmem_limit_bytes=56 * 1024 * 1024
        ),
        name="block",
    )(
        state,
        land_mask.T,
        cotangent,
        kernel,
        row(norm_gain),
        row(norm_bias),
        weight_in,
        bias_hidden,
        weight_out.T,
        row(bias_out),
        row(layer_scale),
    )
    factor = 1.0 / math.sqrt(ROWS * nlat * COLS * nlon)
    shape = lambda *s: jax.ShapeDtypeStruct(s, F32)
    outs = pl.pallas_call(
        functools.partial(finish_kernel, factor, size, mrows, erows),
        out_shape=(
            jax.ShapeDtypeStruct((ROWS, COLS, C), BF16),
            jax.ShapeDtypeStruct((ROWS, COLS, C), BF16),
            shape(7, 7, C),
            shape(1, C),
            shape(1, C),
            shape(C, HID),
            shape(HID),
            shape(C, HID),
            shape(1, C),
            shape(1, C),
        ),
        in_specs=[hbm] * 3,
        out_specs=(hbm,) * 2 + (vmem,) * 8,
        scratch_shapes=[
            pltpu.VMEM((2, size, mrows + erows, 128), BF16),
            pltpu.VMEM((size * erows, 128), F32),
            dma((3,)),
        ],
        compiler_params=pltpu.CompilerParams(vmem_limit_bytes=56 * 1024 * 1024),
        name="finish",
    )(total, block, grad)
    outs = [o.reshape(-1) if o.shape[0] == 1 else o for o in outs]
    outs[7] = outs[7].T
    return tuple(outs)


def solution(mesh):
    cells, plane, whole = P("lat", "lon", None), P("lat", "lon"), P()
    return jax.shard_map(
        functools.partial(on_device, mesh.shape["lon"], mesh.shape["lat"]),
        mesh=mesh,
        in_specs=(cells, plane, cells) + (whole,) * 8,
        out_specs=(cells, cells) + (whole,) * 8,
        check_vma=False,
    )
```

time: 102 us -> 90.8 us (0.89)
  local copies, waits for them, and re-layouts: 5.94 us -> 0 us
  Pallas kernels: 94.4 us -> 90 us
    pallas_call x1, Pallas kernels: 93.2 us -> 71.9 us  [on_device(): pl.pallas_call(functools.partial(main_kernel, nlon, nlat), out_shape=(jax...]
    pallas_call x1, Pallas kernels: 1.28 us -> 18 us  [on_device(): pl.pallas_call(functools.partial(finish_kernel, factor, size, mrows, erow...]
    unnamed x22 -> x0, local copies, waits for them, and re-layouts: 5.94 us -> none
where the time goes in v2:
time: 90.8 us; the launch traced here: 90.6 us
  Pallas kernels  90 us (99%)
    pallas_call x1, Pallas kernels, on_device(): pl.pallas_call(functools.partial(main_kernel, nlon, nlat), out_shape=(jax...  71.9 us
    pallas_call x1, Pallas kernels, on_device(): pl.pallas_call(functools.partial(finish_kernel, factor, size, mrows, erow...  18 us

profile of v2, /device:TPU:1, one launch (start us, length us, event | category | flops | bytes accessed | tf_op | source)
XLA Modules:
  0.0 90.6 jit_solution(1939134797929579371)
XLA Ops:
  0.6 71.9 %block.1 = (bf16[32,16,192]{2,1,0:T(8,128)(2,1)}, bf16[32,16,192]{2,1,0:T(8,128)(2,1)}, bf16[2,32,48,128]{3,2,1,0:T(8,128)(2,1)}) custom-call(bf16[32,16,192]{2,1,0:T(8,128)(2,1)} %state_h.1, s32[16,32]{1,0:T(8,128)} %bitcast.12, bf16[32,16,192]{2,1,0:T(8,128)(2,1)} %cot_h.1, bf16[7,7,192]{2,1,0:T(8,128)(2,1)} %kern_h.1, f32[1,192]{1,0:T(1,128)} %bitcast.13, ...), custom_call_target="tpu_custom_call" | custom-call | tf_op jit(solution)/shard_map/block/pallas_call | solution.py:680
  72.6 18.0 %finish.1 = (bf16[32,16,192]{2,1,0:T(8,128)(2,1)}, bf16[32,16,192]{2,1,0:T(8,128)(2,1)}, f32[7,7,192]{2,1,0:T(8,128)}, f32[1,192]{1,0:T(1,128)}, f32[1,192]{1,0:...) custom-call(bf16[2,32,48,128]{3,2,1,0:T(8,128)(2,1)} %get-tuple-elem, ...), custom_call_target="tpu_custom_call" | custom-call | tf_op jit(solution)/shard_map/finish/pallas_call | solution.py:762

commit v3 on v2

--- a/solution.py
+++ b/solution.py
@@ -622,13 +622,13 @@
 
 
 def finish_kernel(
-    factor, size, mrows, erows, total_h, block, grad,
+    factor, size, mrows, erows, total_h, block_h, grad_h,
     block_out, grad_out, gk, gg, gb, gw_in, gbh, gw_out, gbo, gls, total, extra, sem,
 ):
     moves = [
         pltpu.make_async_copy(src, dst, sem.at[i])
         for i, (src, dst) in enumerate(
-            ((total_h, total), (block, block_out), (grad, grad_out))
+            ((total_h, total), (block_h, block_out), (grad_h, grad_out))
         )
     ]
     for move in moves:
@@ -774,7 +774,7 @@
             shape(1, C),
         ),
         in_specs=[hbm] * 3,
-        out_specs=(hbm,) * 2 + (vmem,) * 8,
+        out_specs=(vmem,) * 10,
         scratch_shapes=[
             pltpu.VMEM((2, size, mrows + erows, 128), BF16),
             pltpu.VMEM((size * erows, 128), F32),

time: 90.8 us -> 75.3 us (0.83)
  Pallas kernels: 90 us -> 74.5 us
    pallas_call x1, Pallas kernels: 18 us -> 2.58 us  [on_device(): pl.pallas_call(functools.partial(finish_kernel, factor, size, mrows, erow...]
where the time goes in v3:
time: 75.3 us; the launch traced here: 75.2 us
  Pallas kernels  74.5 us (99%)
    pallas_call x1, Pallas kernels, on_device(): pl.pallas_call(functools.partial(main_kernel, nlon, nlat), out_shape=(jax...  71.9 us
    pallas_call x1, Pallas kernels, on_device(): pl.pallas_call(functools.partial(finish_kernel, factor, size, mrows, erow...  2.58 us

profile of v3, /device:TPU:1, one launch (start us, length us, event | category | flops | bytes accessed | tf_op | source)
XLA Modules:
  0.0 75.2 jit_solution(16114953011084450189)
XLA Ops:
  0.6 71.9 %block.1 = (bf16[32,16,192]{2,1,0:T(8,128)(2,1)}, bf16[32,16,192]{2,1,0:T(8,128)(2,1)}, bf16[2,32,48,128]{3,2,1,0:T(8,128)(2,1)}) custom-call(bf16[32,16,192]{2,1,0:T(8,128)(2,1)} %state_h.1, s32[16,32]{1,0:T(8,128)} %bitcast.12, bf16[32,16,192]{2,1,0:T(8,128)(2,1)} %cot_h.1, bf16[7,7,192]{2,1,0:T(8,128)(2,1)} %kern_h.1, f32[1,192]{1,0:T(1,128)} %bitcast.13, ...), custom_call_target="tpu_custom_call" | custom-call | tf_op jit(solution)/shard_map/block/pallas_call | solution.py:680
  72.6 2.6 %finish.1 = (bf16[32,16,192]{2,1,0:T(8,128)(2,1)}, bf16[32,16,192]{2,1,0:T(8,128)(2,1)}, f32[7,7,192]{2,1,0:T(8,128)}, f32[1,192]{1,0:T(1,128)}, f32[1,192]{1,0:...) custom-call(bf16[2,32,48,128]{3,2,1,0:T(8,128)(2,1)} %get-tuple-elem, ...), custom_call_target="tpu_custom_call" | custom-call | tf_op jit(solution)/shard_map/finish/pallas_call | solution.py:762

commit v4 on v3

--- a/solution.py
+++ b/solution.py
@@ -94,6 +94,8 @@
     shiftq,
     taps,
     maskb,
+    mixp,
+    ghid_s,
     normed_s,
     precot_s,
     hidden_s,
@@ -112,6 +114,8 @@
     extra,
     pay,
     xrecv,
+    payx,
+    xrecvx,
     zslot,
     abuf,
     fin,
@@ -123,10 +127,14 @@
     core_r,
     xs,
     xr,
+    xsx,
+    xrx,
     zs,
     zr,
     xas,
     xar,
+    ls,
+    lr,
 ):
     px, nzl, nzh, py = groups(nlon, nlat)
     size, nz, mrows, erows = shares(nlon, nlat)
@@ -196,6 +204,32 @@
         def _(r):
             for b in range(7):
                 out[b, r] = field[r, 5 + b : 21 + b, :].reshape(2, 8, C)
+
+    def inner(b, h):
+        return b >= 3 if h == 0 else b <= 3
+
+    def shift_some(r, wanted):
+        for b in range(7):
+            for h in range(2):
+                if wanted(b, h):
+                    shifted[b, r, h] = pad[r, 5 + b + 8 * h : 13 + b + 8 * h, :]
+
+    def conv_half(r0, h, wanted, acc):
+        for b in range(7):
+            for a in range(7):
+                if wanted(b, h):
+                    acc = acc + shifted[b, pl.ds(r0 + a, 4), h] * taps[a * 7 + b]
+        return acc
+
+    def conv_inner(r0):
+        for h in range(2):
+            mixp[pl.ds(r0, 4), h] = conv_half(r0, h, inner, jnp.zeros((4, 8, C), F32))
+
+    def conv_outer(r0):
+        halves = [
+            conv_half(r0, h, lambda b, h: not inner(b, h), mixp[pl.ds(r0, 4), h]) for h in range(2)
+        ]
+        return jnp.stack(halves, axis=1).reshape(4 * COLS, C)
 
     def conv_rows(source, r0, rows, flip):
         acc = jnp.zeros((rows, 2, 8, C), F32)
@@ -394,8 +428,34 @@
     send_halo(0)
     for load in loads[3:]:
         load.wait()
+
+    ct_all = cot[...].astype(F32) * maskb[...]
+    gb_all = (ct_all * scale[...].reshape(1, 1, C)).reshape(CELLS, C)
+    bcot_s[...] = gb_all.astype(BF16)
+    sums[2] = jnp.sum(gb_all.reshape(CELLS // 8, 8, C), axis=0)
+    for t in range(HID // 256):
+        wide = slice(256 * t, 256 * t + 256)
+        ghid_s[:, wide] = dot(bcot_s[...], w_out[:, wide])
+
+    @pl.loop(3, 3 + ROWS)
+    def _(r):
+        shift_some(r, inner)
+
+    @pl.loop(1, ROWS // 4 - 1)
+    def _(i):
+        conv_inner(4 * i)
+
     take_halo(0, pad)
-    shift(pad, shifted)
+
+    @pl.loop(3, 3 + ROWS)
+    def _(r):
+        shift_some(r, lambda b, h: not inner(b, h))
+
+    for q in range(3):
+        shift_some(q, lambda b, h: True)
+        shift_some(ROWS + 3 + q, lambda b, h: True)
+    conv_inner(0)
+    conv_inner(ROWS - 4)
 
     block = 8
     cells = block * COLS
@@ -405,7 +465,7 @@
         r0 = blk * block
         here = pl.ds(pl.multiple_of(r0 * COLS, cells), cells)
         mixed = jnp.concatenate(
-            [conv_rows(shifted, r0 + 4 * i, 4, False).reshape(4 * COLS, C) for i in range(block // 4)],
+            [conv_outer(r0 + 4 * i) for i in range(block // 4)],
             axis=0,
         )
         average = jnp.sum(mixed, axis=1, keepdims=True) * (1.0 / C)
@@ -430,10 +490,7 @@
         block_out[rows_here] = (
             (sea_w * (st + scale[...] * branch)).astype(BF16).reshape(block, COLS, C)
         )
-        grad_branch = ct * scale[...]
-        bcot = grad_branch.astype(BF16)
-        bcot_s[here, :] = bcot
-        grad_pre = dot(bcot, w_out[...]) * slope
+        grad_pre = ghid_s[here, :] * slope
         precot = grad_pre.astype(BF16)
         precot_s[here, :] = precot
         grad_normed = dot(precot, w_in[...], ((1,), (1,)))
@@ -450,7 +507,6 @@
 
         sums[0] += fold8(grad_normed * unit)
         sums[1] += fold8(grad_normed)
-        sums[2] += fold8(grad_branch)
         sums[3] += fold8(ct * branch)
         sumh[...] += fold8(grad_pre)
 
@@ -474,9 +530,8 @@
     pair_w = to_pair(0, pl.ds(0, WROWS))
     pair_w.start()
 
-    for b in range(7):
-
-        def step(i, accs, b=b):
+    def kernel_grad(b):
+        def step(i, accs):
             r0 = i * 4
             m = padq[pl.ds(3 + r0, 4), 8:24, :].reshape(4, 2, 8, C)
             return tuple(
@@ -487,6 +542,34 @@
         accs = lax.fori_loop(0, ROWS // 4, step, tuple(jnp.zeros((8, C), F32) for _ in range(7)))
         for a in range(7):
             small[a * 7 + b : a * 7 + b + 1, 0:C] = jnp.sum(accs[a], axis=0, keepdims=True)
+
+    for b in range(3):
+        kernel_grad(b)
+
+    def group_copy(k, sender):
+        return remote("group", pay.at[k], xrecv.at[sender], xs.at[k], xr.at[sender], in_group(k))
+
+    def rest_copy(k, sender):
+        return remote("group", payx.at[k], xrecvx.at[sender], xsx.at[k], xrx.at[sender], in_group(k))
+
+    pair_w.wait()
+
+    def add_pair(k):
+        rows = pl.ds(pl.multiple_of(k * mrows, 32), mrows)
+        both = wbuf[core, rows, :] + wrecv[rows, :]
+        psum[rows, :] = both
+        pay[k] = both.astype(BF16)
+
+    add_pair(me)
+
+    @pl.loop(1, size)
+    def _(d):
+        k = lax.rem(me + d, size)
+        add_pair(k)
+        group_copy(k, me).start()
+
+    for b in range(3, 7):
+        kernel_grad(b)
     for i in range(4):
         small[49 + i : 50 + i, 0:C] = jnp.sum(sums[i], axis=0, keepdims=True)
     hid_row = jnp.sum(sumh[...], axis=0, keepdims=True)
@@ -497,15 +580,6 @@
     pair_s = to_pair(1, pl.ds(WROWS, SROWS))
     pair_s.start()
 
-    pair_w.wait()
-
-    @pl.loop(0, size)
-    def _(k):
-        rows = pl.ds(pl.multiple_of(k * mrows, 32), mrows)
-        both = wbuf[core, rows, :] + wrecv[rows, :]
-        psum[rows, :] = both
-        pay[k, 0:mrows, :] = both.astype(BF16)
-
     pair_s.wait()
     rest_w = wbuf[core, MAIN:WROWS, :] + wrecv[MAIN:WROWS, :]
     both = wbuf[core, WROWS:, :] + wrecv[WROWS:, :]
@@ -513,15 +587,12 @@
     other = jnp.concatenate([rest_w, high, both - high], axis=0)
     for i in range((TOT - MAIN) // size):
         extra[pl.ds(i, size, stride=erows), :] = other[i * size : (i + 1) * size]
-    pay[:, mrows:, :] = extra[...].reshape(size, erows, 128).astype(BF16)
-
-    def group_copy(k, sender):
-        return remote("group", pay.at[k], xrecv.at[sender], xs.at[k], xr.at[sender], in_group(k))
+    payx[...] = extra[...].reshape(size, erows, 128).astype(BF16)
 
     @pl.loop(1, size)
     def _(d):
         k = lax.rem(me + d, size)
-        group_copy(k, me).start()
+        rest_copy(k, me).start()
 
     def halves(v):
         first = (WROWS - MAIN) // size
@@ -540,17 +611,23 @@
         k = lax.rem(me + d, size)
         group_copy(k, k).wait()
 
-    def add_chunk(d, acc):
+    def add_main(d, acc):
         return acc + xrecv[lax.rem(me + d, size)].astype(F32)
 
-    mine = jnp.concatenate(
-        [
-            psum[pl.ds(pl.multiple_of(me * mrows, 32), mrows), :],
-            extra[pl.ds(pl.multiple_of(me * erows, 16), erows), :],
-        ],
-        axis=0,
-    )
-    zslot[zi] = halves(lax.fori_loop(1, size, add_chunk, mine))
+    def add_rest(d, acc):
+        return acc + xrecvx[lax.rem(me + d, size)].astype(F32)
+
+    mine = psum[pl.ds(pl.multiple_of(me * mrows, 32), mrows), :]
+    mine = lax.fori_loop(1, size, add_main, mine)
+
+    @pl.loop(1, size)
+    def _(d):
+        k = lax.rem(me + d, size)
+        rest_copy(k, k).wait()
+
+    minex = extra[pl.ds(pl.multiple_of(me * erows, 16), erows), :]
+    minex = lax.fori_loop(1, size, add_rest, minex)
+    zslot[zi] = halves(jnp.concatenate([mine, minex], axis=0))
 
     def z_copy(k, sender):
         return remote("z", zslot.at[sender], zslot.at[sender], zs.at[k], zr.at[sender], in_z(k))
@@ -605,16 +682,24 @@
     def _(d):
         back_copy(me, lax.rem(me + d, size)).start()
 
+    def last_copy(k):
+        return remote("last", abuf.at[k], fin.at[k], ls.at[k], lr.at[k], pair)
+
+    last_copy(me).start()
+
     @pl.loop(1, size)
     def _(d):
         k = lax.rem(me + d, size)
         back_copy(k, k).wait()
-
-    last = remote("last", abuf, fin, core_s.at[2], core_r.at[2], pair)
-    last.start()
+        last_copy(k).start()
+
     own_store = pltpu.make_async_copy(abuf, total.at[core], store_s.at[2])
     own_store.start()
-    last.wait()
+
+    @pl.loop(0, size)
+    def _(k):
+        last_copy(k).wait()
+
     fin_store = pltpu.make_async_copy(fin, total.at[1 - core], store_s.at[3])
     fin_store.start()
     for store in (block_store, grad_store, own_store, fin_store):
@@ -706,6 +791,8 @@
             pltpu.VMEM((7, PADR, 2, 8, C), F32),
             pltpu.VMEM((49, 8, C), F32),
             pltpu.VMEM((ROWS, COLS, C), F32),
+            pltpu.VMEM((ROWS, 2, 8, C), F32),
+            pltpu.VMEM((CELLS, HID), F32),
             pltpu.VMEM((CELLS, C), BF16),
             pltpu.VMEM((CELLS, HID), BF16),
             pltpu.VMEM((CELLS, HID), BF16),
@@ -722,8 +809,10 @@
             pltpu.VMEM((WROWS + SROWS, 128), F32),
             pltpu.VMEM((MAIN, 128), F32),
             pltpu.VMEM((size * erows, 128), F32),
-            pltpu.VMEM((size, mrows + erows, 128), BF16),
-            pltpu.VMEM((size, mrows + erows, 128), BF16),
+            pltpu.VMEM((size, mrows, 128), BF16),
+            pltpu.VMEM((size, mrows, 128), BF16),
+            pltpu.VMEM((size, erows, 128), BF16),
+            pltpu.VMEM((size, erows, 128), BF16),
             pltpu.VMEM((nz, mrows + erows, 128), BF16),
             pltpu.VMEM((size, mrows + erows, 128), BF16),
             pltpu.VMEM((size, mrows + erows, 128), BF16),
@@ -731,12 +820,16 @@
             dma((4,)),
             dma((2, 8)),
             dma((2, 8)),
-            dma((3,)),
-            dma((3,)),
+            dma((2,)),
+            dma((2,)),
+            dma((size,)),
+            dma((size,)),
             dma((size,)),
             dma((size,)),
             dma((nz,)),
             dma((nz,)),
+            dma((size,)),
+            dma((size,)),
             dma((size,)),
             dma((size,)),
         ],

time: 75.3 us -> 74.7 us (level); the launches traced: 75.2 us -> 73.8 us
  Pallas kernels: 74.5 us -> 73.1 us
    pallas_call x1, Pallas kernels: 71.9 us -> 70.5 us  [on_device(): pl.pallas_call(functools.partial(main_kernel, nlon, nlat), out_shape=(jax...]
where the time goes in v4:
time: 74.7 us; the launch traced here: 73.8 us
  Pallas kernels  73.1 us (98%)
    pallas_call x1, Pallas kernels, on_device(): pl.pallas_call(functools.partial(main_kernel, nlon, nlat), out_shape=(jax...  70.5 us
    pallas_call x1, Pallas kernels, on_device(): pl.pallas_call(functools.partial(finish_kernel, factor, size, mrows, erow...  2.58 us

profile of v4, /device:TPU:1, one launch (start us, length us, event | category | flops | bytes accessed | tf_op | source)
XLA Modules:
  0.0 73.8 jit_solution(10627696808251249436)
XLA Ops:
  0.6 70.5 %block.1 = (bf16[32,16,192]{2,1,0:T(8,128)(2,1)}, bf16[32,16,192]{2,1,0:T(8,128)(2,1)}, bf16[2,32,48,128]{3,2,1,0:T(8,128)(2,1)}) custom-call(bf16[32,16,192]{2,1,0:T(8,128)(2,1)} %state_h.1, s32[16,32]{1,0:T(8,128)} %bitcast.12, bf16[32,16,192]{2,1,0:T(8,128)(2,1)} %cot_h.1, bf16[7,7,192]{2,1,0:T(8,128)(2,1)} %kern_h.1, f32[1,192]{1,0:T(1,128)} %bitcast.13, ...), custom_call_target="tpu_custom_call" | custom-call | tf_op jit(solution)/shard_map/block/pallas_call | solution.py:765
  71.2 2.6 %finish.1 = (bf16[32,16,192]{2,1,0:T(8,128)(2,1)}, bf16[32,16,192]{2,1,0:T(8,128)(2,1)}, f32[7,7,192]{2,1,0:T(8,128)}, f32[1,192]{1,0:T(1,128)}, f32[1,192]{1,0:...) custom-call(bf16[2,32,48,128]{3,2,1,0:T(8,128)(2,1)} %get-tuple-elem, ...), custom_call_target="tpu_custom_call" | custom-call | tf_op jit(solution)/shard_map/finish/pallas_call | solution.py:855

commit v5 on v4

--- a/solution.py
+++ b/solution.py
@@ -216,9 +216,10 @@
 
     def conv_half(r0, h, wanted, acc):
         for b in range(7):
-            for a in range(7):
-                if wanted(b, h):
-                    acc = acc + shifted[b, pl.ds(r0 + a, 4), h] * taps[a * 7 + b]
+            if wanted(b, h):
+                win = shifted[b, pl.ds(r0, 10), h]
+                for a in range(7):
+                    acc = acc + win[a : a + 4] * taps[a * 7 + b]
         return acc
 
     def conv_inner(r0):
@@ -234,9 +235,10 @@
     def conv_rows(source, r0, rows, flip):
         acc = jnp.zeros((rows, 2, 8, C), F32)
         for b in range(7):
+            win = source[b, pl.ds(r0, rows + 6)]
             for a in range(7):
                 k = taps[48 - a * 7 - b] if flip else taps[a * 7 + b]
-                acc = acc + source[b, pl.ds(r0 + a, rows)] * k
+                acc = acc + win[a : a + rows] * k
         return acc
 
     barrier = pltpu.get_barrier_semaphore()
@@ -437,7 +439,7 @@
         wide = slice(256 * t, 256 * t + 256)
         ghid_s[:, wide] = dot(bcot_s[...], w_out[:, wide])
 
-    @pl.loop(3, 3 + ROWS)
+    @pl.loop(3, 3 + ROWS, unroll=4)
     def _(r):
         shift_some(r, inner)
 
@@ -447,7 +449,7 @@
 
     take_halo(0, pad)
 
-    @pl.loop(3, 3 + ROWS)
+    @pl.loop(3, 3 + ROWS, unroll=4)
     def _(r):
         shift_some(r, lambda b, h: not inner(b, h))
 
@@ -457,7 +459,7 @@
     conv_inner(0)
     conv_inner(ROWS - 4)
 
-    block = 8
+    block = ROWS
     cells = block * COLS
 
     @pl.loop(0, ROWS // block)
@@ -511,7 +513,6 @@
         sumh[...] += fold8(grad_pre)
 
     pick_halo(1)
-    send_halo(1)
     block_store = pltpu.make_async_copy(block_out, block_h, store_s.at[0])
     block_store.start()
 
@@ -534,8 +535,9 @@
         def step(i, accs):
             r0 = i * 4
             m = padq[pl.ds(3 + r0, 4), 8:24, :].reshape(4, 2, 8, C)
+            win = shifted[b, pl.ds(r0, 10)]
             return tuple(
-                accs[a] + jnp.sum((m * shifted[b, pl.ds(r0 + a, 4)]).reshape(8, 8, C), axis=0)
+                accs[a] + jnp.sum((m * win[a : a + 4]).reshape(8, 8, C), axis=0)
                 for a in range(7)
             )
 
@@ -562,11 +564,16 @@
 
     add_pair(me)
 
-    @pl.loop(1, size)
-    def _(d):
-        k = lax.rem(me + d, size)
+    def far(i, n, first):
+        return 1 + lax.rem(i + first, n - 1)
+
+    @pl.loop(0, size - 1)
+    def _(i):
+        k = lax.rem(me + far(i, size, size * 5 // 8 - 1), size)
         add_pair(k)
         group_copy(k, me).start()
+
+    send_halo(1)
 
     for b in range(3, 7):
         kernel_grad(b)
@@ -589,9 +596,9 @@
         extra[pl.ds(i, size, stride=erows), :] = other[i * size : (i + 1) * size]
     payx[...] = extra[...].reshape(size, erows, 128).astype(BF16)
 
-    @pl.loop(1, size)
-    def _(d):
-        k = lax.rem(me + d, size)
+    @pl.loop(0, size - 1)
+    def _(i):
+        k = lax.rem(me + far(i, size, size * 5 // 8 - 1), size)
         rest_copy(k, me).start()
 
     def halves(v):
@@ -632,17 +639,17 @@
     def z_copy(k, sender):
         return remote("z", zslot.at[sender], zslot.at[sender], zs.at[k], zr.at[sender], in_z(k))
 
-    @pl.loop(1, nz)
-    def _(d):
-        z_copy(lax.rem(zi + d, nz), zi).start()
+    @pl.loop(0, nz - 1)
+    def _(i):
+        z_copy(lax.rem(zi + far(i, nz, nz // 2 - 1), nz), zi).start()
 
     take_halo(1, padq)
     shift(padq, shiftq)
 
-    @pl.loop(0, ROWS // 4)
+    @pl.loop(0, ROWS // 2)
     def _(i):
-        rows_here = pl.ds(i * 4, 4)
-        grad = conv_rows(shiftq, i * 4, 4, True).reshape(4, COLS, C)
+        rows_here = pl.ds(i * 2, 2)
+        grad = conv_rows(shiftq, i * 2, 2, True).reshape(2, COLS, C)
         grad_state[rows_here] = (
             maskb[rows_here] * (cot[rows_here].astype(F32) + grad)
         ).astype(BF16)
@@ -678,9 +685,9 @@
     def back_copy(owner, k):
         return remote("back", abuf.at[owner], abuf.at[owner], xas.at[k], xar.at[owner], in_group(k))
 
-    @pl.loop(1, size)
-    def _(d):
-        back_copy(me, lax.rem(me + d, size)).start()
+    @pl.loop(0, size - 1)
+    def _(i):
+        back_copy(me, lax.rem(me + far(i, size, size * 5 // 8 - 1), size)).start()
 
     def last_copy(k):
         return remote("last", abuf.at[k], fin.at[k], ls.at[k], lr.at[k], pair)

time: 74.7 us -> 77.7 us (1.040); the launches traced: 73.8 us -> 77.6 us
  Pallas kernels: 73.1 us -> 76.9 us
    pallas_call x1, Pallas kernels: 70.5 us -> 74.4 us  [on_device(): pl.pallas_call(functools.partial(main_kernel, nlon, nlat), out_shape=(jax...]
where the time goes in v5:
time: 77.7 us; the launch traced here: 77.6 us
  Pallas kernels  76.9 us (99%)
    pallas_call x1, Pallas kernels, on_device(): pl.pallas_call(functools.partial(main_kernel, nlon, nlat), out_shape=(jax...  74.4 us
    pallas_call x1, Pallas kernels, on_device(): pl.pallas_call(functools.partial(finish_kernel, factor, size, mrows, erow...  2.58 us

profile of v5, /device:TPU:1, one launch (start us, length us, event | category | flops | bytes accessed | tf_op | source)
XLA Modules:
  0.0 77.6 jit_solution(13855398469740489788)
XLA Ops:
  0.6 74.4 %block.1 = (bf16[32,16,192]{2,1,0:T(8,128)(2,1)}, bf16[32,16,192]{2,1,0:T(8,128)(2,1)}, bf16[2,32,48,128]{3,2,1,0:T(8,128)(2,1)}) custom-call(bf16[32,16,192]{2,1,0:T(8,128)(2,1)} %state_h.1, s32[16,32]{1,0:T(8,128)} %bitcast.12, bf16[32,16,192]{2,1,0:T(8,128)(2,1)} %cot_h.1, bf16[7,7,192]{2,1,0:T(8,128)(2,1)} %kern_h.1, f32[1,192]{1,0:T(1,128)} %bitcast.13, ...), custom_call_target="tpu_custom_call" | custom-call | tf_op jit(solution)/shard_map/block/pallas_call | solution.py:772
  75.0 2.6 %finish.1 = (bf16[32,16,192]{2,1,0:T(8,128)(2,1)}, bf16[32,16,192]{2,1,0:T(8,128)(2,1)}, f32[7,7,192]{2,1,0:T(8,128)}, f32[1,192]{1,0:T(1,128)}, f32[1,192]{1,0:...) custom-call(bf16[2,32,48,128]{3,2,1,0:T(8,128)(2,1)} %get-tuple-elem, ...), custom_call_target="tpu_custom_call" | custom-call | tf_op jit(solution)/shard_map/finish/pallas_call | solution.py:862

commit v6 on v5

--- a/solution.py
+++ b/solution.py
@@ -513,6 +513,7 @@
         sumh[...] += fold8(grad_pre)
 
     pick_halo(1)
+    send_halo(1)
     block_store = pltpu.make_async_copy(block_out, block_h, store_s.at[0])
     block_store.start()
 
@@ -572,8 +573,6 @@
         k = lax.rem(me + far(i, size, size * 5 // 8 - 1), size)
         add_pair(k)
         group_copy(k, me).start()
-
-    send_halo(1)
 
     for b in range(3, 7):
         kernel_grad(b)
@@ -642,6 +641,28 @@
     @pl.loop(0, nz - 1)
     def _(i):
         z_copy(lax.rem(zi + far(i, nz, nz // 2 - 1), nz), zi).start()
+
+    @pl.loop(1, nz)
+    def _(d):
+        k = lax.rem(zi + d, nz)
+        z_copy(k, k).wait()
+
+    whole = zslot[0].astype(F32)
+    for k in range(1, nz):
+        whole = whole + zslot[k].astype(F32)
+    abuf[me] = halves(whole)
+
+    def back_copy(owner, k):
+        return remote("back", abuf.at[owner], abuf.at[owner], xas.at[k], xar.at[owner], in_group(k))
+
+    @pl.loop(0, size - 1)
+    def _(i):
+        back_copy(me, lax.rem(me + far(i, size, size * 5 // 8 - 1), size)).start()
+
+    def last_copy(k):
+        return remote("last", abuf.at[k], fin.at[k], ls.at[k], lr.at[k], pair)
+
+    last_copy(me).start()
 
     take_halo(1, padq)
     shift(padq, shiftq)
@@ -671,28 +692,6 @@
 
     grad_store = pltpu.make_async_copy(grad_state, grad_h, store_s.at[1])
     grad_store.start()
-
-    @pl.loop(1, nz)
-    def _(d):
-        k = lax.rem(zi + d, nz)
-        z_copy(k, k).wait()
-
-    whole = zslot[0].astype(F32)
-    for k in range(1, nz):
-        whole = whole + zslot[k].astype(F32)
-    abuf[me] = halves(whole)
-
-    def back_copy(owner, k):
-        return remote("back", abuf.at[owner], abuf.at[owner], xas.at[k], xar.at[owner], in_group(k))
-
-    @pl.loop(0, size - 1)
-    def _(i):
-        back_copy(me, lax.rem(me + far(i, size, size * 5 // 8 - 1), size)).start()
-
-    def last_copy(k):
-        return remote("last", abuf.at[k], fin.at[k], ls.at[k], lr.at[k], pair)
-
-    last_copy(me).start()
 
     @pl.loop(1, size)
     def _(d):

time: 77.7 us -> 72.8 us (0.937)
  Pallas kernels: 76.9 us -> 72 us
    pallas_call x1, Pallas kernels: 74.4 us -> 69.4 us  [on_device(): pl.pallas_call(functools.partial(main_kernel, nlon, nlat), out_shape=(jax...]
where the time goes in v6:
time: 72.8 us; the launch traced here: 72.7 us
  Pallas kernels  72 us (99%)
    pallas_call x1, Pallas kernels, on_device(): pl.pallas_call(functools.partial(main_kernel, nlon, nlat), out_shape=(jax...  69.4 us
    pallas_call x1, Pallas kernels, on_device(): pl.pallas_call(functools.partial(finish_kernel, factor, size, mrows, erow...  2.58 us

profile of v6, /device:TPU:1, one launch (start us, length us, event | category | flops | bytes accessed | tf_op | source)
XLA Modules:
  0.0 72.7 jit_solution(10614930400894499115)
XLA Ops:
  0.6 69.4 %block.1 = (bf16[32,16,192]{2,1,0:T(8,128)(2,1)}, bf16[32,16,192]{2,1,0:T(8,128)(2,1)}, bf16[2,32,48,128]{3,2,1,0:T(8,128)(2,1)}) custom-call(bf16[32,16,192]{2,1,0:T(8,128)(2,1)} %state_h.1, s32[16,32]{1,0:T(8,128)} %bitcast.12, bf16[32,16,192]{2,1,0:T(8,128)(2,1)} %cot_h.1, bf16[7,7,192]{2,1,0:T(8,128)(2,1)} %kern_h.1, f32[1,192]{1,0:T(1,128)} %bitcast.13, ...), custom_call_target="tpu_custom_call" | custom-call | tf_op jit(solution)/shard_map/block/pallas_call | solution.py:771
  70.1 2.6 %finish.1 = (bf16[32,16,192]{2,1,0:T(8,128)(2,1)}, bf16[32,16,192]{2,1,0:T(8,128)(2,1)}, f32[7,7,192]{2,1,0:T(8,128)}, f32[1,192]{1,0:T(1,128)}, f32[1,192]{1,0:...) custom-call(bf16[2,32,48,128]{3,2,1,0:T(8,128)(2,1)} %get-tuple-elem, ...), custom_call_target="tpu_custom_call" | custom-call | tf_op jit(solution)/shard_map/finish/pallas_call | solution.py:861
